TPU v7x, 32 devices: a whole 2x2x4 slice. The times are simulated.
32 devices in a mesh: groups: 2 (over x), seq: 16 (over z, y, core).
Axes of the slice: x: 2, y: 2, z: 4, core: 2. Of those that a mesh axis runs over, the one named last changes fastest.
Arguments:
- clip_tokens: bfloat16 [32, 128, 512], P(('groups', 'seq')), parts along dimension 0, may hold values from -6 to 6
- spatial_qkv: bfloat16 [512, 1536], replicated, may hold values from -4.6403883 to 4.6403883
- spatial_out: bfloat16 [512, 512], replicated, may hold values from -0.5 to 0.5
- temporal_qkv: bfloat16 [512, 1536], replicated, may hold values from -4.6403883 to 4.6403883
- temporal_out: bfloat16 [512, 512], replicated, may hold values from -0.5 to 0.5
- mlp_up: bfloat16 [512, 2048], replicated, may hold values from -0.25 to 0.25
- mlp_down: bfloat16 [2048, 512], replicated, may hold values from -0.25 to 0.25
Outputs:
- layer_out: bfloat16 [32, 128, 512], P(('groups', 'seq')), parts along dimension 0
There are 2 independent parts, one for each index of `groups`. A program takes and returns all parts, laid end to end along the dimension named above; an argument that names none is the same for every part. Nothing has to cross between parts.
All inputs are finite; a program needn't handle non-finite values.
Results may differ from a plain program's by a relative error of at most 0.013.
Values may be sent and summed in bfloat16 or wider, within the bound.
No kernel may reach another device: no remote copies, remote signals or barrier semaphores. Data moves between devices by JAX's collectives and lax.ppermute only.
A program may use at most 128 MiB of HBM per device.

v0:
```python
import jax
import jax.numpy as jnp
from jax import lax
from jax.sharding import PartitionSpec as P

HEADS = 8


def norm_rows(values):
    center = values - jnp.mean(values, axis=-1, keepdims=True)
    spread = jnp.mean(center * center, axis=-1, keepdims=True)
    return (center * lax.rsqrt(spread + 1e-05)).astype(jnp.bfloat16)


def softmax_rows(scores):
    row_max = jnp.max(scores, axis=-1, keepdims=True)
    raised = jnp.exp(scores - row_max)
    return (raised / jnp.sum(raised, axis=-1, keepdims=True)).astype(jnp.bfloat16)


def spatial_frame(frame_rows, w_qkv, w_out):
    patches, model_width = frame_rows.shape
    head_width = model_width // HEADS
    packed = jnp.dot(
        norm_rows(frame_rows.astype(jnp.float32)), w_qkv, preferred_element_type=jnp.float32
    )
    packed = packed.astype(jnp.bfloat16).reshape(patches, 3, HEADS, head_width)
    key_rows = packed[:, 1]
    value_rows = packed[:, 2]
    block_rows = min(512, patches)
    query_rows = packed[:, 0].reshape(patches // block_rows, block_rows, HEADS, head_width)

    def one_block(query_block):
        scores = jnp.einsum(
            "qhd,khd->hqk", query_block, key_rows, preferred_element_type=jnp.float32
        ) * head_width ** (-0.5)
        weights = softmax_rows(scores)
        attended = jnp.einsum(
            "hqk,khd->qhd", weights, value_rows, preferred_element_type=jnp.float32
        )
        return attended.astype(jnp.bfloat16).reshape(block_rows, model_width)

    attended = lax.map(one_block, query_rows).reshape(patches, model_width)
    merged = frame_rows.astype(jnp.float32) + jnp.dot(
        attended, w_out, preferred_element_type=jnp.float32
    )
    return merged.astype(jnp.bfloat16)


def temporal_block(tokens, w_qkv, w_out):
    frames, count_rows, model_width = tokens.shape
    head_width = model_width // HEADS
    flat_rows = tokens.reshape(frames * count_rows, model_width)
    packed = jnp.dot(
        norm_rows(flat_rows.astype(jnp.float32)), w_qkv, preferred_element_type=jnp.float32
    )
    packed = packed.astype(jnp.bfloat16).reshape(frames, count_rows, 3, HEADS, head_width)
    scores = jnp.einsum(
        "fkhd,gkhd->khfg", packed[:, :, 0], packed[:, :, 1], preferred_element_type=jnp.float32
    ) * head_width ** (-0.5)
    weights = softmax_rows(scores)
    attended = jnp.einsum(
        "khfg,gkhd->fkhd", weights, packed[:, :, 2], preferred_element_type=jnp.float32
    )
    attended = attended.astype(jnp.bfloat16).reshape(frames * count_rows, model_width)
    merged = flat_rows.astype(jnp.float32) + jnp.dot(
        attended, w_out, preferred_element_type=jnp.float32
    )
    return merged.astype(jnp.bfloat16)


def feed_forward(tokens, w_up, w_down):
    raised = jnp.dot(
        norm_rows(tokens.astype(jnp.float32)), w_up, preferred_element_type=jnp.float32
    )
    hidden = jax.nn.gelu(raised, approximate=True).astype(jnp.bfloat16)
    merged = tokens.astype(jnp.float32) + jnp.dot(
        hidden, w_down, preferred_element_type=jnp.float32
    )
    return merged.astype(jnp.bfloat16)


def local(clip_tokens, spatial_qkv, spatial_out, temporal_qkv, temporal_out, mlp_up, mlp_down):
    frame_count, patches, model_width = clip_tokens.shape
    devices = lax.axis_size("seq")
    mixed = lax.map(
        lambda frame_rows: spatial_frame(frame_rows, spatial_qkv, spatial_out), clip_tokens
    )
    blocks = mixed.reshape(frame_count, devices, patches // devices, model_width)
    arrived = lax.all_to_all(blocks, "seq", split_axis=1, concat_axis=0, tiled=True)
    frames = arrived.shape[0]
    count_rows = arrived.shape[2]
    tokens = arrived.reshape(frames, count_rows, model_width)
    after_time = temporal_block(tokens, temporal_qkv, temporal_out)
    returned = after_time.reshape(frames, 1, count_rows, model_width)
    arrived_back = lax.all_to_all(returned, "seq", split_axis=0, concat_axis=1, tiled=True)
    result_rows = arrived_back.reshape(frame_count * patches, model_width)
    result_rows = feed_forward(result_rows, mlp_up, mlp_down)
    return result_rows.reshape(frame_count, patches, model_width)


def solution(mesh):
    in_specs = (P(("groups", "seq"), None, None), P(), P(), P(), P(), P(), P())
    out_specs = P(("groups", "seq"), None, None)
    return jax.shard_map(local, mesh=mesh, in_specs=in_specs, out_specs=out_specs, check_vma=False)
```

profile of v0, /device:TPU:0, one launch (start us, length us, event | category | flops | bytes accessed | tf_op | source)
XLA Modules:
  0.0 44.2 jit_solution(6778775718888962342)
XLA Ops:
  0.0 1.2 %convert_reduce_fusion.2 = f32[128]{0:T(128)S(1)} fusion(bf16[1,128,512]{2,1,0:T(8,128)(2,1)} %param.7), kind=kLoop, calls=%fused_computation.45 | loop fusion | flops 130944 | bytes 131584 | tf_op jit(solution)/shard_map/while/body/eval_jaxpr/reduce_sum | solution.py:10
  1.2 1.1 %fusion.31 = f32[128]{0:T(128)S(1)} fusion(bf16[1,128,512]{2,1,0:T(8,128)(2,1)} %param.7, f32[128]{0:T(128)S(1)} %broadcast_multiply_fusion.2), kind=kLoop, calls=%fused_computation.50 | loop fusion | flops 262016 | bytes 132096 | tf_op jit(solution)/shard_map/while/body/eval_jaxpr/reduce_sum | solution.py:11
  2.3 1.9 %convolution_convert_fusion.1 = bf16[128,1536]{1,0:T(8,128)(2,1)S(1)} fusion(bf16[512,1536]{1,0:T(8,128)(2,1)} %param.8, bf16[1,128,512]{2,1,0:T(8,128)(2,1)} %param.7, f32[128]{0:T(128)S(1)} %add_rsqrt_fusion.2, f32[128]{0:T(128)S(1)} %broadcast_multiply_fusion.2), kind=kOutput, calls=%fused_computation.3 | convolution fusion | flops 201785344 | bytes 2098176 | tf_op jit(solution)/shard_map/while/body/eval_jaxpr/dot_general | solution.py:24
  4.2 0.2 copy.23
  4.4 0.0 copy-start.1
  4.4 0.0 copy-start.2
  4.4 0.4 fusion.67
  4.8 1.1 %convolution_multiply_fusion = f32[8,128,128]{1,2,0:T(8,128)} fusion(bf16[128,3,8,64]{0,3,2,1:T(8,128)(2,1)S(1)} %bitcast.104), kind=kOutput, calls=%fused_computation.9 | convolution fusion | flops 16908288 | bytes 786432 | tf_op jit(solution)/shard_map/while/body/eval_jaxpr/while/body/eval_jaxpr/qhd,khd->hqk/dot_general | solution.py:34
  5.9 1.5 %convolution_convert_fusion.3 = bf16[8,64,128]{2,1,0:T(8,128)(2,1)S(1)} fusion(f32[8,128]{1,0:T(8,128)S(1)} %fusion.67, bf16[128,3,8,64]{0,3,2,1:T(8,128)(2,1)S(1)} %bitcast.105, f32[8,128,128]{1,2,0:T(8,128)} %convolution_multiply_fusion), kind=kOutput, calls=%fused_computation.19 | convolution fusion | flops 17237120 | bytes 1314816 | tf_op jit(solution)/shard_map/while/body/eval_jaxpr/while/body/eval_jaxpr/hqk,khd->qhd/dot_general | solution.py:38
  7.4 0.0 copy-done.1
  7.4 0.0 copy-done.2
  7.4 0.3 fusion.12
  7.6 15.1 %all_to_all.8 = bf16[1,16,8,512]{3,2,0,1:T(8,128)(2,1)S(1)} all-to-all(bf16[1,16,8,512]{3,2,0,1:T(8,128)(2,1)S(1)} %fusion.12), channel_id=1, replica_groups=mesh['groups'=2,'seq'=16] {'seq'}, dimensions={1} | all-to-all | bytes 262144 | tf_op jit(solution)/shard_map/all_to_all | solution.py:90
  22.8 0.1 convert_reduce_fusion.1
  22.9 0.1 div.53
  23.0 0.2 fusion.38
  23.2 0.1 rsqrt.33
  23.2 1.8 %convolution_convert_fusion = bf16[128,1536]{1,0:T(8,128)(2,1)S(1)} fusion(bf16[512,1536]{1,0:T(8,128)(2,1)} %param.10, bf16[1,16,8,512]{3,2,0,1:T(8,128)(2,1)S(1)} %all_to_all.8, f32[128]{0:T(128)S(1)} %rsqrt.33, f32[128]{0:T(128)S(1)} %div.53), kind=kOutput, calls=%fused_computation.2 | convolution fusion | flops 201785344 | bytes 2098176 | tf_op jit(solution)/shard_map/dot_general | solution.py:54
  25.1 0.4 %reshape.151 = bf16[16,8,3,8,64]{4,3,2,1,0:T(8,128)(2,1)S(1)} reshape(bf16[128,1536]{1,0:T(8,128)(2,1)S(1)} %convolution_convert_fusion) | data formatting | bytes 786432 | tf_op jit(solution)/shard_map/reshape | solution.py:57
  25.5 0.9 %fusion.66 = (bf16[16,8,1,8,64]{4,3,2,1,0:T(8,128)(2,1)S(1)}, bf16[16,8,1,8,64]{4,3,2,1,0:T(8,128)(2,1)}, bf16[16,8,1,8,64]{4,3,2,1,0:T(8,128)(2,1)S(1)}) fusion(bf16[16,8,3,8,64]{4,3,2,1,0:T(8,128)(2,1)S(1)} %reshape.151), kind=kLoop, calls=%fused_computation.88 | loop fusion | bytes 786432 | tf_op jit(solution)/shard_map/slice | solution.py:59
  26.5 1.1 %fusion.68 = f32[8,8,16]{2,1,0:T(8,128)} fusion(bf16[16,8,1,8,64]{4,3,2,1,0:T(8,128)(2,1)S(1)} %get-tuple-element.40, bf16[16,8,1,8,64]{4,3,2,1,0:T(8,128)(2,1)S(1)} %get-tuple-element.33), kind=kOutput, calls=%fused_computation.90 | convolution fusion | flops 2146319 | bytes 266240 | tf_op jit(solution)/shard_map/sub | solution.py:17
  27.6 0.4 convolution_multiply_fusion.1
  28.0 1.4 %fusion.6 = bf16[16,8,8,64]{3,0,2,1:T(8,128)(2,1)S(1)} fusion(bf16[16,8,1,8,64]{4,3,2,1,0:T(8,128)(2,1)} %get-tuple-element.34, f32[8,8,16]{2,1,0:T(8,128)} %fusion.68, f32[8,8,16,16]{2,3,1,0:T(8,128)S(1)} %convolution_multiply_fusion.1), kind=kOutput, calls=%fused_computation.12 | convolution fusion | flops 2212879 | bytes 331776 | tf_op jit(solution)/shard_map/khfg,gkhd->fkhd/dot_general | solution.py:62
  29.4 0.1 copy.30
  29.5 0.2 reshape.152
  29.7 0.2 fusion.11
  30.0 10.5 %all_to_all.9 = bf16[16,1,8,512]{3,2,1,0:T(8,128)(2,1)S(1)} all-to-all(bf16[16,1,8,512]{3,2,1,0:T(8,128)(2,1)S(1)} %fusion.11), channel_id=1, replica_groups=mesh['groups'=2,'seq'=16] {'seq'}, dimensions={0} | all-to-all | bytes 262144 | tf_op jit(solution)/shard_map/all_to_all | solution.py:96
  40.5 0.1 convert_reduce_fusion
  40.6 0.1 div.58
  40.7 0.2 fusion.40
  40.9 0.1 rsqrt.35
  41.0 3.2 %fusion.10 = bf16[1,128,512]{2,1,0:T(8,128)(2,1)} fusion(bf16[2048,512]{1,0:T(8,128)(2,1)S(1)} %copy-done, bf16[16,1,8,512]{3,2,1,0:T(8,128)(2,1)S(1)} %all_to_all.9, bf16[512,2048]{1,0:T(8,128)(2,1)} %param.12, f32[128]{0:T(128)S(1)} %rsqrt.35, f32[128]{0:T(128)S(1)} %div.58), kind=kOutput, calls=%fused_computation.20 | convolution fusion | flops 539688960 | bytes 4457472 | tf_op jit(solution)/shard_map/dot_general | solution.py:77
  (10 shorter events, 0.0 us)
Async XLA Ops:
  0.0 41.0 %copy-start = (bf16[2048,512]{1,0:T(8,128)(2,1)S(1)}, bf16[2048,512]{1,0:T(8,128)(2,1)}, u32[]{:S(2)}) copy-start(bf16[2048,512]{1,0:T(8,128)(2,1)} %param.13) | copy-start | bytes 6291460
  4.4 2.9 %copy-start.1 = (bf16[1,128,512]{2,1,0:T(8,128)(2,1)S(1)}, bf16[1,128,512]{2,1,0:T(8,128)(2,1)}, u32[]{:S(2)}) copy-start(bf16[1,128,512]{2,1,0:T(8,128)(2,1)} %param.7) | copy-start | bytes 393220
  4.4 2.9 %copy-start.2 = (bf16[512,512]{1,0:T(8,128)(2,1)S(1)}, bf16[512,512]{1,0:T(8,128)(2,1)}, u32[]{:S(2)}) copy-start(bf16[512,512]{1,0:T(8,128)(2,1)} %param.9) | copy-start | bytes 1572868
  28.0 1.7 %copy-start.3 = (bf16[512,512]{1,0:T(8,128)(2,1)S(1)}, bf16[512,512]{1,0:T(8,128)(2,1)}, u32[]{:S(2)}) copy-start(bf16[512,512]{1,0:T(8,128)(2,1)} %param.11) | copy-start | bytes 1572868
where the time goes:
time: 44.5 us; the launch traced here: 44.2 us
  blocking collectives  25.6 us (58%)
  matrix products  13.3 us (30%)
  other arithmetic  2.81 us (6%)
  local copies, waits for them, and re-layouts  2.23 us (5%)
    all_to_all x1, blocking collectives, local(): lax.all_to_all(blocks, 'seq', split_axis=1, concat_axis=0, tiled=True)  15.1 us
    all_to_all x1, blocking collectives, local(): lax.all_to_all(returned, 'seq', split_axis=0, concat_axis=1, tiled=True)  10.5 us
    dot_general x1, matrix products, feed_forward(): jnp.dot(hidden, w_down, preferred_element_type=jnp.float32)  3.19 us
    dot_general x1, matrix products, spatial_frame(): jnp.dot(norm_rows(frame_rows.astype(jnp.float32)), w_qkv, preferred_eleme...  1.9 us
    dot_general x1, matrix products, temporal_block(): jnp.dot(norm_rows(flat_rows.astype(jnp.float32)), w_qkv, preferred_elemen...  1.82 us
    sub x2, matrix products, softmax_rows(): raised = jnp.exp(scores - row_max)  1.51 us
    dot_general x1, matrix products, one_block(): jnp.einsum('hqk,khd->qhd', weights, value_rows, preferred_element_type=jn...  1.47 us
    reduce_sum x3, other arithmetic, norm_rows(): spread = jnp.mean(center * center, axis=-1, keepdims=True)  1.43 us

commit v1 on v0

v1 whole, which is shorter than its diff:
```python
import functools

import jax
import jax.numpy as jnp
from jax import lax
from jax.experimental import pallas as pl
from jax.experimental.pallas import tpu as pltpu
from jax.sharding import PartitionSpec as P

HEADS = 8
LANES = 128
BF16 = jnp.bfloat16
F32 = jnp.float32
VMEM_LIMIT = 48 * 1024 * 1024


def norm_rows(values):
    center = values - jnp.mean(values, axis=-1, keepdims=True)
    spread = jnp.mean(center * center, axis=-1, keepdims=True)
    return (center * lax.rsqrt(spread + 1e-05)).astype(BF16)


def attend_block(packed_ref, heads_ref, start, block, stride, width):
    rows = packed_ref.shape[0]
    head = width // HEADS
    pair = 2 * head
    scale = head ** (-0.5) * 1.4426950408889634
    low_q = lax.broadcasted_iota(jnp.int32, (block, pair), 1) < head
    low_v = lax.broadcasted_iota(jnp.int32, (rows, pair), 1) < head
    ones = jnp.concatenate(
        [jnp.where(low_v, 1.0, 0.0), jnp.where(low_v, 0.0, 1.0)], axis=0
    ).astype(BF16)
    if stride:
        query_at = start + lax.broadcasted_iota(jnp.int32, (2 * block, rows), 0)
        key_at = lax.broadcasted_iota(jnp.int32, (2 * block, rows), 1)
        same = lax.rem(query_at, stride) == lax.rem(key_at, stride)
    for at in range(0, width, pair):
        query = packed_ref[pl.ds(start, block), at : at + pair]
        key = packed_ref[:, width + at : width + at + pair]
        value = packed_ref[:, 2 * width + at : 2 * width + at + pair]
        zero_q = jnp.zeros_like(query)
        both = jnp.concatenate(
            [jnp.where(low_q, query, zero_q), jnp.where(low_q, zero_q, query)], axis=0
        )
        scores = lax.dot_general(both, key, (((1,), (1,)), ((), ())), preferred_element_type=F32)
        if stride:
            scores = jnp.where(same, scores, -jnp.inf)
        top = jnp.max(scores, axis=-1, keepdims=True)
        raised = jnp.exp2((scores - top) * scale).astype(BF16)
        side = jnp.concatenate([raised[:block], raised[block:]], axis=1)
        zero_v = jnp.zeros_like(value)
        values = jnp.concatenate(
            [jnp.where(low_v, value, zero_v), jnp.where(low_v, zero_v, value)], axis=0
        )
        total = jnp.dot(
            side, jnp.concatenate([values, ones], axis=1), preferred_element_type=F32
        )
        heads_ref[pl.ds(start, block), at : at + pair] = (
            total[:, :pair] / total[:, pair:]
        ).astype(BF16)


def attention_kernel(stride, x_ref, qkv_ref, out_ref, y_ref, packed_ref, heads_ref):
    rows, width = x_ref.shape
    normed = norm_rows(x_ref[...].astype(F32))
    packed_ref[...] = jnp.dot(normed, qkv_ref[...], preferred_element_type=F32).astype(BF16)
    block = min(rows, LANES)
    if rows == block:
        attend_block(packed_ref, heads_ref, 0, block, stride, width)
    else:

        @pl.loop(0, rows // block)
        def _(index):
            start = pl.multiple_of(index * block, block)
            attend_block(packed_ref, heads_ref, start, block, stride, width)

    y_ref[...] = (
        x_ref[...].astype(F32)
        + jnp.dot(heads_ref[...], out_ref[...], preferred_element_type=F32)
    ).astype(BF16)


def attention_layer(rows, w_qkv, w_out, stride):
    count, width = rows.shape
    return pl.pallas_call(
        functools.partial(attention_kernel, stride),
        out_shape=jax.ShapeDtypeStruct((count, width), BF16),
        in_specs=[pl.BlockSpec(memory_space=pltpu.VMEM)] * 3,
        out_specs=pl.BlockSpec(memory_space=pltpu.VMEM),
        scratch_shapes=[
            pltpu.VMEM((count, 3 * width), BF16),
            pltpu.VMEM((count, width), BF16),
        ],
        compiler_params=pltpu.CompilerParams(vmem_limit_bytes=VMEM_LIMIT),
    )(rows, w_qkv, w_out)


def mlp_block(x, up_ref, down_ref, piece):
    normed = norm_rows(x.astype(F32))
    total = x.astype(F32)
    for at in range(0, up_ref.shape[1], piece):
        u = jnp.dot(normed, up_ref[:, at : at + piece], preferred_element_type=F32)
        half = 0.5 * u
        bend = jnp.tanh(u * (0.7978845608028654 + 0.035677408136300125 * (u * u)))
        hidden = (half + half * bend).astype(BF16)
        total += jnp.dot(hidden, down_ref[at : at + piece, :], preferred_element_type=F32)
    return total.astype(BF16)


def mlp_kernel(x_ref, up_ref, down_ref, y_ref):
    rows = x_ref.shape[0]
    block = min(rows, LANES)
    piece = min(512, up_ref.shape[1])
    if rows == block:
        y_ref[...] = mlp_block(x_ref[...], up_ref, down_ref, piece)
    else:

        @pl.loop(0, rows // block)
        def _(index):
            here = pl.ds(pl.multiple_of(index * block, block), block)
            y_ref[here, :] = mlp_block(x_ref[here, :], up_ref, down_ref, piece)


def mlp_layer(rows, w_up, w_down):
    return pl.pallas_call(
        mlp_kernel,
        out_shape=jax.ShapeDtypeStruct(rows.shape, BF16),
        in_specs=[pl.BlockSpec(memory_space=pltpu.VMEM)] * 3,
        out_specs=pl.BlockSpec(memory_space=pltpu.VMEM),
        compiler_params=pltpu.CompilerParams(vmem_limit_bytes=VMEM_LIMIT),
    )(rows, w_up, w_down)


def local(clip_tokens, spatial_qkv, spatial_out, temporal_qkv, temporal_out, mlp_up, mlp_down):
    frame_count, patches, width = clip_tokens.shape
    devices = lax.axis_size("seq")
    share = patches // devices
    frames = frame_count * devices
    mixed = jnp.stack(
        [attention_layer(clip_tokens[i], spatial_qkv, spatial_out, 0) for i in range(frame_count)]
    )
    blocks = mixed.reshape(frame_count, devices, share, width)
    arrived = lax.all_to_all(blocks, "seq", split_axis=1, concat_axis=0, tiled=True)
    tokens = arrived.reshape(frames * share, width)
    after_time = attention_layer(tokens, temporal_qkv, temporal_out, share)
    returned = after_time.reshape(frames, 1, share, width)
    back = lax.all_to_all(returned, "seq", split_axis=0, concat_axis=1, tiled=True)
    result = mlp_layer(back.reshape(frame_count * patches, width), mlp_up, mlp_down)
    return result.reshape(frame_count, patches, width)


def solution(mesh):
    in_specs = (P(("groups", "seq"), None, None), P(), P(), P(), P(), P(), P())
    out_specs = P(("groups", "seq"), None, None)
    return jax.shard_map(local, mesh=mesh, in_specs=in_specs, out_specs=out_specs, check_vma=False)
```

time: 44.5 us -> 36.3 us (0.82)
  matrix products: 13.3 us -> 0 us
  Pallas kernels: 0 us -> 4.37 us
  local copies, waits for them, and re-layouts: 2.23 us -> 5.81 us
  other arithmetic: 2.81 us -> 0 us
    dot_general x9 -> x0, matrix products: 11.8 us -> none  [the longest x1 3.19 us: feed_forward(): jnp.dot(hidden, w_down, preferred_element_type=jnp.float32)]
    unnamed x8 -> x14, local copies, waits for them, and re-layouts: 0.02 us -> 5.81 us
    pallas_call x0 -> x3, Pallas kernels: none -> 4.37 us  [the longest x2 2.27 us: attention_layer(): pl.pallas_call(functools.partial(attention_kernel, stride), out_shape=jax...]
    reduce_sum x6 -> x0, other arithmetic: 2.78 us -> none  [the longest x3 1.43 us: norm_rows(): spread = jnp.mean(center * center, axis=-1, keepdims=True)]
    sub x2 -> x0, matrix products: 1.51 us -> none  [softmax_rows(): raised = jnp.exp(scores - row_max)]
    slice x1 -> x0, local copies, waits for them, and re-layouts: 0.93 us -> none  [temporal_block(): packed[:, :, 0]]
    reshape x2 -> x0, local copies, waits for them, and re-layouts: 0.66 us -> none  [the longest x1 0.45 us: temporal_block(): packed.astype(jnp.bfloat16)]
where the time goes in v1:
time: 36.3 us; the launch traced here: 36 us
  blocking collectives  25.8 us (71%)
  local copies, waits for them, and re-layouts  5.81 us (16%)
  Pallas kernels  4.37 us (12%)
    all_to_all x1, blocking collectives, local(): lax.all_to_all(blocks, 'seq', split_axis=1, concat_axis=0, tiled=True)  15.3 us
    all_to_all x1, blocking collectives, local(): lax.all_to_all(returned, 'seq', split_axis=0, concat_axis=1, tiled=True)  10.5 us
    unnamed x14, local copies, waits for them, and re-layouts  5.81 us
    pallas_call x2, Pallas kernels, attention_layer(): pl.pallas_call(functools.partial(attention_kernel, stride), out_shape=jax...  2.27 us
    pallas_call x1, Pallas kernels, mlp_layer(): pl.pallas_call(mlp_kernel, out_shape=jax.ShapeDtypeStruct(rows.shape, BF1...  2.1 us

profile of v1, /device:TPU:0, one launch (start us, length us, event | category | flops | bytes accessed | tf_op | source)
XLA Modules:
  0.0 36.0 jit_solution(520423020845555688)
XLA Ops:
  0.0 0.0 copy-start.2
  0.0 1.4 %copy-done.2 = bf16[512,1536]{1,0:T(8,128)(2,1)S(1)} copy-done((bf16[512,1536]{1,0:T(8,128)(2,1)S(1)}, bf16[512,1536]{1,0:T(8,128)(2,1)}, u32[]{:S(2)}) %copy-start.2) | copy-done | bytes 1572888
  1.4 0.0 copy-start.4
  1.4 1.0 %copy-done.4 = bf16[512,512]{1,0:T(8,128)(2,1)S(1)} copy-done((bf16[512,512]{1,0:T(8,128)(2,1)S(1)}, bf16[512,512]{1,0:T(8,128)(2,1)}, u32[]{:S(2)}) %copy-start.4) | copy-done | bytes 524312
  2.5 0.0 copy-start.6
  2.5 0.9 %copy-done.6 = bf16[1,128,512]{2,1,0:T(8,128)(2,1)S(1)} copy-done((bf16[1,128,512]{2,1,0:T(8,128)(2,1)S(1)}, bf16[1,128,512]{2,1,0:T(8,128)(2,1)}, u32[]{:S(2)}) %copy-start.6) | copy-done | bytes 131096
  3.4 0.0 copy-start
  3.4 0.0 copy-start.1
  3.4 1.1 %shard_map.73 = bf16[128,512]{1,0:T(8,128)(2,1)S(1)} custom-call(bf16[128,512]{1,0:T(8,128)(2,1)S(1)} %bitcast.14, bf16[512,1536]{1,0:T(8,128)(2,1)S(1)} %copy-done.2, bf16[512,512]{1,0:T(8,128)(2,1)S(1)} %copy-done.4), custom_call_target="tpu_custom_call" | custom-call | tf_op jit(solution)/shard_map/pallas_call | solution.py:85
  4.5 15.3 %all_to_all.8 = bf16[1,16,8,512]{3,2,0,1:T(8,128)(2,1)S(1)} all-to-all(bf16[1,16,8,512]{3,2,0,1:T(8,128)(2,1)S(1)} %bitcast.13), channel_id=1, replica_groups=mesh['groups'=2,'seq'=16] {'seq'}, dimensions={1} | all-to-all | bytes 262144 | tf_op jit(solution)/shard_map/all_to_all | solution.py:143
  19.8 0.0 copy-start.3
  19.8 1.4 %copy-done.3 = bf16[512,1536]{1,0:T(8,128)(2,1)S(1)} copy-done((bf16[512,1536]{1,0:T(8,128)(2,1)S(1)}, bf16[512,1536]{1,0:T(8,128)(2,1)}, u32[]{:S(2)}) %copy-start.3) | copy-done | bytes 1572888
  21.2 0.0 copy-start.5
  21.2 1.0 %copy-done.5 = bf16[512,512]{1,0:T(8,128)(2,1)S(1)} copy-done((bf16[512,512]{1,0:T(8,128)(2,1)S(1)}, bf16[512,512]{1,0:T(8,128)(2,1)}, u32[]{:S(2)}) %copy-start.5) | copy-done | bytes 524312
  22.2 1.1 %shard_map.74 = bf16[128,512]{1,0:T(8,128)(2,1)S(1)} custom-call(bf16[128,512]{1,0:T(8,128)(2,1)S(1)} %bitcast.10, bf16[512,1536]{1,0:T(8,128)(2,1)S(1)} %copy-done.3, bf16[512,512]{1,0:T(8,128)(2,1)S(1)} %copy-done.5), custom_call_target="tpu_custom_call" | custom-call | tf_op jit(solution)/shard_map/pallas_call | solution.py:85
  23.4 10.5 %all_to_all.9 = bf16[16,1,8,512]{3,2,1,0:T(8,128)(2,1)S(1)} all-to-all(bf16[16,1,8,512]{3,2,1,0:T(8,128)(2,1)S(1)} %bitcast.11), channel_id=1, replica_groups=mesh['groups'=2,'seq'=16] {'seq'}, dimensions={0} | all-to-all | bytes 262144 | tf_op jit(solution)/shard_map/all_to_all | solution.py:147
  33.9 0.0 copy-done
  33.9 0.0 copy-done.1
  33.9 2.1 %shard_map.75 = bf16[128,512]{1,0:T(8,128)(2,1)} custom-call(bf16[128,512]{1,0:T(8,128)(2,1)S(1)} %bitcast.12, bf16[512,2048]{1,0:T(8,128)(2,1)S(1)} %copy-done, bf16[2048,512]{1,0:T(8,128)(2,1)S(1)} %copy-done.1), custom_call_target="tpu_custom_call" | custom-call | tf_op jit(solution)/shard_map/pallas_call | solution.py:125
Async XLA Ops:
  0.0 1.4 %copy-start.2 = (bf16[512,1536]{1,0:T(8,128)(2,1)S(1)}, bf16[512,1536]{1,0:T(8,128)(2,1)}, u32[]{:S(2)}) copy-start(bf16[512,1536]{1,0:T(8,128)(2,1)} %qkv_ref.2) | copy-start | bytes 4718596
  1.4 1.0 %copy-start.4 = (bf16[512,512]{1,0:T(8,128)(2,1)S(1)}, bf16[512,512]{1,0:T(8,128)(2,1)}, u32[]{:S(2)}) copy-start(bf16[512,512]{1,0:T(8,128)(2,1)} %out_ref.2) | copy-start | bytes 1572868
  2.5 0.9 %copy-start.6 = (bf16[1,128,512]{2,1,0:T(8,128)(2,1)S(1)}, bf16[1,128,512]{2,1,0:T(8,128)(2,1)}, u32[]{:S(2)}) copy-start(bf16[1,128,512]{2,1,0:T(8,128)(2,1)} %param.7) | copy-start | bytes 393220
  3.4 30.5 %copy-start = (bf16[512,2048]{1,0:T(8,128)(2,1)S(1)}, bf16[512,2048]{1,0:T(8,128)(2,1)}, u32[]{:S(2)}) copy-start(bf16[512,2048]{1,0:T(8,128)(2,1)} %up_ref.1) | copy-start | bytes 6291460
  3.4 30.5 %copy-start.1 = (bf16[2048,512]{1,0:T(8,128)(2,1)S(1)}, bf16[2048,512]{1,0:T(8,128)(2,1)}, u32[]{:S(2)}) copy-start(bf16[2048,512]{1,0:T(8,128)(2,1)} %down_ref.1) | copy-start | bytes 6291460
  19.8 1.4 %copy-start.3 = (bf16[512,1536]{1,0:T(8,128)(2,1)S(1)}, bf16[512,1536]{1,0:T(8,128)(2,1)}, u32[]{:S(2)}) copy-start(bf16[512,1536]{1,0:T(8,128)(2,1)} %qkv_ref.3) | copy-start | bytes 4718596
  21.2 1.0 %copy-start.5 = (bf16[512,512]{1,0:T(8,128)(2,1)S(1)}, bf16[512,512]{1,0:T(8,128)(2,1)}, u32[]{:S(2)}) copy-start(bf16[512,512]{1,0:T(8,128)(2,1)} %out_ref.3) | copy-start | bytes 1572868

commit v2 on v1

--- a/solution.py
+++ b/solution.py
@@ -11,7 +11,11 @@
 LANES = 128
 BF16 = jnp.bfloat16
 F32 = jnp.float32
-VMEM_LIMIT = 48 * 1024 * 1024
+MIB = 1024 * 1024
+
+
+def vmem_limit(rows):
+    return 10 * MIB + rows * 32 * 1024
 
 
 def norm_rows(values):
@@ -60,10 +64,8 @@
         ).astype(BF16)
 
 
-def attention_kernel(stride, x_ref, qkv_ref, out_ref, y_ref, packed_ref, heads_ref):
+def attend_rows(stride, x_ref, out_ref, y_ref, packed_ref, heads_ref):
     rows, width = x_ref.shape
-    normed = norm_rows(x_ref[...].astype(F32))
-    packed_ref[...] = jnp.dot(normed, qkv_ref[...], preferred_element_type=F32).astype(BF16)
     block = min(rows, LANES)
     if rows == block:
         attend_block(packed_ref, heads_ref, 0, block, stride, width)
@@ -80,10 +82,75 @@
     ).astype(BF16)
 
 
-def attention_layer(rows, w_qkv, w_out, stride):
+def spatial_kernel(
+    x_hbm, qkv_hbm, out_hbm, next_qkv_hbm, next_out_hbm,
+    y_ref, next_qkv_ref, next_out_ref,
+    x_ref, qkv_ref, out_ref, packed_ref, heads_ref, sems,
+):
+    width = x_ref.shape[1]
+    fetch_x = pltpu.make_async_copy(x_hbm, x_ref, sems.at[0])
+    fetch_x.start()
+    parts = []
+    for part in range(3):
+        columns = slice(part * width, (part + 1) * width)
+        copy = pltpu.make_async_copy(
+            qkv_hbm.at[:, columns], qkv_ref.at[:, columns], sems.at[part + 1]
+        )
+        copy.start()
+        parts.append((columns, copy))
+    fetch_out = pltpu.make_async_copy(out_hbm, out_ref, sems.at[4])
+    fetch_out.start()
+    fetch_next_qkv = pltpu.make_async_copy(next_qkv_hbm, next_qkv_ref, sems.at[5])
+    fetch_next_qkv.start()
+    fetch_next_out = pltpu.make_async_copy(next_out_hbm, next_out_ref, sems.at[6])
+    fetch_next_out.start()
+    fetch_x.wait()
+    normed = norm_rows(x_ref[...].astype(F32))
+    for columns, copy in parts:
+        copy.wait()
+        packed_ref[:, columns] = jnp.dot(
+            normed, qkv_ref[:, columns], preferred_element_type=F32
+        ).astype(BF16)
+    fetch_out.wait()
+    attend_rows(0, x_ref, out_ref, y_ref, packed_ref, heads_ref)
+    fetch_next_qkv.wait()
+    fetch_next_out.wait()
+
+
+def spatial_layer(rows, w_qkv, w_out, next_qkv, next_out):
+    count, width = rows.shape
+    operands = (rows, w_qkv, w_out, next_qkv, next_out)
+    return pl.pallas_call(
+        spatial_kernel,
+        out_shape=[
+            jax.ShapeDtypeStruct((count, width), BF16),
+            jax.ShapeDtypeStruct(next_qkv.shape, BF16),
+            jax.ShapeDtypeStruct(next_out.shape, BF16),
+        ],
+        in_specs=[pl.BlockSpec(memory_space=pltpu.HBM)] * len(operands),
+        out_specs=[pl.BlockSpec(memory_space=pltpu.VMEM)] * 3,
+        scratch_shapes=[
+            pltpu.VMEM(rows.shape, BF16),
+            pltpu.VMEM(w_qkv.shape, BF16),
+            pltpu.VMEM(w_out.shape, BF16),
+            pltpu.VMEM((count, 3 * width), BF16),
+            pltpu.VMEM((count, width), BF16),
+            pltpu.SemaphoreType.DMA((7,)),
+        ],
+        compiler_params=pltpu.CompilerParams(vmem_limit_bytes=vmem_limit(count)),
+    )(*(pltpu.with_memory_space_constraint(each, pltpu.HBM) for each in operands))
+
+
+def temporal_kernel(stride, x_ref, qkv_ref, out_ref, y_ref, packed_ref, heads_ref):
+    normed = norm_rows(x_ref[...].astype(F32))
+    packed_ref[...] = jnp.dot(normed, qkv_ref[...], preferred_element_type=F32).astype(BF16)
+    attend_rows(stride, x_ref, out_ref, y_ref, packed_ref, heads_ref)
+
+
+def temporal_layer(rows, w_qkv, w_out, stride):
     count, width = rows.shape
     return pl.pallas_call(
-        functools.partial(attention_kernel, stride),
+        functools.partial(temporal_kernel, stride),
         out_shape=jax.ShapeDtypeStruct((count, width), BF16),
         in_specs=[pl.BlockSpec(memory_space=pltpu.VMEM)] * 3,
         out_specs=pl.BlockSpec(memory_space=pltpu.VMEM),
@@ -91,7 +158,7 @@
             pltpu.VMEM((count, 3 * width), BF16),
             pltpu.VMEM((count, width), BF16),
         ],
-        compiler_params=pltpu.CompilerParams(vmem_limit_bytes=VMEM_LIMIT),
+        compiler_params=pltpu.CompilerParams(vmem_limit_bytes=vmem_limit(count)),
     )(rows, w_qkv, w_out)
 
 
@@ -127,7 +194,7 @@
         out_shape=jax.ShapeDtypeStruct(rows.shape, BF16),
         in_specs=[pl.BlockSpec(memory_space=pltpu.VMEM)] * 3,
         out_specs=pl.BlockSpec(memory_space=pltpu.VMEM),
-        compiler_params=pltpu.CompilerParams(vmem_limit_bytes=VMEM_LIMIT),
+        compiler_params=pltpu.CompilerParams(vmem_limit_bytes=vmem_limit(rows.shape[0])),
     )(rows, w_up, w_down)
 
 
@@ -136,13 +203,17 @@
     devices = lax.axis_size("seq")
     share = patches // devices
     frames = frame_count * devices
-    mixed = jnp.stack(
-        [attention_layer(clip_tokens[i], spatial_qkv, spatial_out, 0) for i in range(frame_count)]
-    )
+    mixed = []
+    for index in range(frame_count):
+        rows, next_qkv, next_out = spatial_layer(
+            clip_tokens[index], spatial_qkv, spatial_out, temporal_qkv, temporal_out
+        )
+        mixed.append(rows)
+    mixed = jnp.stack(mixed)
     blocks = mixed.reshape(frame_count, devices, share, width)
     arrived = lax.all_to_all(blocks, "seq", split_axis=1, concat_axis=0, tiled=True)
     tokens = arrived.reshape(frames * share, width)
-    after_time = attention_layer(tokens, temporal_qkv, temporal_out, share)
+    after_time = temporal_layer(tokens, next_qkv, next_out, share)
     returned = after_time.reshape(frames, 1, share, width)
     back = lax.all_to_all(returned, "seq", split_axis=0, concat_axis=1, tiled=True)
     result = mlp_layer(back.reshape(frame_count * patches, width), mlp_up, mlp_down)

time: 36.3 us -> 32 us (0.88)
  local copies, waits for them, and re-layouts: 5.81 us -> 0.01 us
  Pallas kernels: 4.37 us -> 5.95 us
    unnamed x14 -> x4, local copies, waits for them, and re-layouts: 5.81 us -> 0.01 us
    pallas_call x2, Pallas kernels: 2.27 us -> 3.85 us  [the longest x1 2.71 us: spatial_layer(): pl.pallas_call(spatial_kernel, out_shape=[jax.ShapeDtypeStruct((count, wi...]
where the time goes in v2:
time: 32 us; the launch traced here: 31.8 us
  blocking collectives  25.8 us (81%)
  Pallas kernels  5.95 us (19%)
    all_to_all x1, blocking collectives, local(): lax.all_to_all(blocks, 'seq', split_axis=1, concat_axis=0, tiled=True)  15.3 us
    all_to_all x1, blocking collectives, local(): lax.all_to_all(returned, 'seq', split_axis=0, concat_axis=1, tiled=True)  10.5 us
    pallas_call x1, Pallas kernels, spatial_layer(): pl.pallas_call(spatial_kernel, out_shape=[jax.ShapeDtypeStruct((count, wi...  2.71 us
    pallas_call x1, Pallas kernels, mlp_layer(): pl.pallas_call(mlp_kernel, out_shape=jax.ShapeDtypeStruct(rows.shape, BF1...  2.1 us
    pallas_call x1, Pallas kernels, temporal_layer(): pl.pallas_call(functools.partial(temporal_kernel, stride), out_shape=jax....  1.14 us

profile of v2, /device:TPU:0, one launch (start us, length us, event | category | flops | bytes accessed | tf_op | source)
XLA Modules:
  0.0 31.8 jit_solution(11148026050001971442)
XLA Ops:
  0.0 0.0 copy-start.1
  0.0 2.7 %shard_map.73 = (bf16[128,512]{1,0:T(8,128)(2,1)S(1)}, bf16[512,1536]{1,0:T(8,128)(2,1)S(1)}, bf16[512,512]{1,0:T(8,128)(2,1)S(1)}) custom-call(bf16[128,512]{1,0:T(8,128)(2,1)} %bitcast.14, bf16[512,1536]{1,0:T(8,128)(2,1)} %qkv_hbm.1, bf16[512,512]{1,0:T(8,128)(2,1)} %out_hbm.1, bf16[512,1536]{1,0:T(8,128)(2,1)} %next_qkv_hbm.1, bf16[512,512]{1,0:T(8,128)(2,1)} %next_out_hbm.1), custom_call_target="tpu_custom_call" | custom-call | tf_op jit(solution)/shard_map/pallas_call | solution.py:123
  2.7 0.0 copy-start
  2.7 15.3 %all_to_all.8 = bf16[1,16,8,512]{3,2,0,1:T(8,128)(2,1)S(1)} all-to-all(bf16[1,16,8,512]{3,2,0,1:T(8,128)(2,1)S(1)} %bitcast.13), channel_id=1, replica_groups=mesh['groups'=2,'seq'=16] {'seq'}, dimensions={1} | all-to-all | bytes 262144 | tf_op jit(solution)/shard_map/all_to_all | solution.py:214
  18.0 1.1 %shard_map.74 = bf16[128,512]{1,0:T(8,128)(2,1)S(1)} custom-call(bf16[128,512]{1,0:T(8,128)(2,1)S(1)} %bitcast.10, bf16[512,1536]{1,0:T(8,128)(2,1)S(1)} %get-tuple-element.9.qkv_ref, bf16[512,512]{1,0:T(8,128)(2,1)S(1)} %get-tuple-element.10.out_ref), custom_call_target="tpu_custom_call" | custom-call | tf_op jit(solution)/shard_map/pallas_call | solution.py:152
  19.1 10.5 %all_to_all.9 = bf16[16,1,8,512]{3,2,1,0:T(8,128)(2,1)S(1)} all-to-all(bf16[16,1,8,512]{3,2,1,0:T(8,128)(2,1)S(1)} %bitcast.11), channel_id=1, replica_groups=mesh['groups'=2,'seq'=16] {'seq'}, dimensions={0} | all-to-all | bytes 262144 | tf_op jit(solution)/shard_map/all_to_all | solution.py:218
  29.7 0.0 copy-done.1
  29.7 0.0 copy-done
  29.7 2.1 %shard_map.75 = bf16[128,512]{1,0:T(8,128)(2,1)} custom-call(bf16[128,512]{1,0:T(8,128)(2,1)S(1)} %bitcast.12, bf16[512,2048]{1,0:T(8,128)(2,1)S(1)} %copy-done, bf16[2048,512]{1,0:T(8,128)(2,1)S(1)} %copy-done.1), custom_call_target="tpu_custom_call" | custom-call | tf_op jit(solution)/shard_map/pallas_call | solution.py:192
Async XLA Ops:
  0.0 29.7 %copy-start.1 = (bf16[2048,512]{1,0:T(8,128)(2,1)S(1)}, bf16[2048,512]{1,0:T(8,128)(2,1)}, u32[]{:S(2)}) copy-start(bf16[2048,512]{1,0:T(8,128)(2,1)} %down_ref.1) | copy-start | bytes 6291460
  2.7 26.9 %copy-start = (bf16[512,2048]{1,0:T(8,128)(2,1)S(1)}, bf16[512,2048]{1,0:T(8,128)(2,1)}, u32[]{:S(2)}) copy-start(bf16[512,2048]{1,0:T(8,128)(2,1)} %up_ref.1) | copy-start | bytes 6291460

commit v3 on v2

v3 whole, which is shorter than its diff:
```python
import functools

import jax
import jax.numpy as jnp
from jax import lax
from jax.experimental import pallas as pl
from jax.experimental.pallas import tpu as pltpu
from jax.sharding import PartitionSpec as P

HEADS = 8
LANES = 128
SUBLANES = 8
BF16 = jnp.bfloat16
F32 = jnp.float32
MIB = 1024 * 1024


def vmem_limit(rows):
    return 10 * MIB + rows * 32 * 1024


def params(rows):
    return pltpu.CompilerParams(vmem_limit_bytes=vmem_limit(rows))


def in_hbm(*arrays):
    return tuple(pltpu.with_memory_space_constraint(each, pltpu.HBM) for each in arrays)


def vmem(count):
    return [pl.BlockSpec(memory_space=pltpu.VMEM)] * count


def norm_rows(values):
    center = values - jnp.mean(values, axis=-1, keepdims=True)
    spread = jnp.mean(center * center, axis=-1, keepdims=True)
    return (center * lax.rsqrt(spread + 1e-05)).astype(BF16)


def dot(left, right):
    return jnp.dot(left, right, preferred_element_type=F32)


def pair_ones(keys, head):
    low = lax.broadcasted_iota(jnp.int32, (keys, 2 * head), 1) < head
    return jnp.concatenate(
        [jnp.where(low, 1.0, 0.0), jnp.where(low, 0.0, 1.0)], axis=0
    ).astype(BF16)


def attend_pair(query, key, value, ones, same):
    block, pair = query.shape
    head = pair // 2
    scale = head ** (-0.5) * 1.4426950408889634
    low_q = lax.broadcasted_iota(jnp.int32, query.shape, 1) < head
    low_v = lax.broadcasted_iota(jnp.int32, value.shape, 1) < head
    zero_q, zero_v = jnp.zeros_like(query), jnp.zeros_like(value)
    both = jnp.concatenate(
        [jnp.where(low_q, query, zero_q), jnp.where(low_q, zero_q, query)], axis=0
    )
    scores = lax.dot_general(both, key, (((1,), (1,)), ((), ())), preferred_element_type=F32)
    if same is not None:
        scores = jnp.where(same, scores, -jnp.inf)
    top = jnp.max(scores, axis=-1, keepdims=True)
    raised = jnp.exp2((scores - top) * scale).astype(BF16)
    side = jnp.concatenate([raised[:block], raised[block:]], axis=1)
    values = jnp.concatenate(
        [jnp.where(low_v, value, zero_v), jnp.where(low_v, zero_v, value)], axis=0
    )
    total = dot(side, jnp.concatenate([values, ones], axis=1))
    return (total[:, :pair] / total[:, pair:]).astype(BF16)


def same_modulo(queries, keys, stride, start=0):
    query_at = start + lax.broadcasted_iota(jnp.int32, (2 * queries, keys), 0)
    key_at = lax.broadcasted_iota(jnp.int32, (2 * queries, keys), 1)
    return lax.rem(query_at, stride) == lax.rem(key_at, stride)


def attend_rows(packed_ref, heads_ref, stride):
    rows, width = heads_ref.shape
    pair = 2 * (width // HEADS)
    block = min(rows, LANES)
    ones = pair_ones(rows, pair // 2)

    def one_block(start):
        same = same_modulo(block, rows, stride, start) if stride else None
        for at in range(0, width, pair):
            heads_ref[pl.ds(start, block), at : at + pair] = attend_pair(
                packed_ref[pl.ds(start, block), at : at + pair],
                packed_ref[:, width + at : width + at + pair],
                packed_ref[:, 2 * width + at : 2 * width + at + pair],
                ones,
                same,
            )

    if rows == block:
        one_block(0)
    else:

        @pl.loop(0, rows // block)
        def _(index):
            one_block(pl.multiple_of(index * block, block))


def blocks_by_distance(x_ref, chips):
    size = x_ref.shape[0] // chips
    mine = lax.axis_index("seq") // 2
    return jnp.concatenate(
        [
            x_ref[pl.ds(pl.multiple_of((mine ^ distance) * size, size), size), :]
            for distance in range(chips)
        ],
        axis=0,
    )


def split_near(rows, chips):
    size = rows.shape[0] // chips
    parts = [rows[at * size : (at + 1) * size] for at in range(chips)]
    return jnp.concatenate(parts[0::2], axis=0), jnp.concatenate(parts[1::2], axis=0)


def spatial_kernel(
    chips,
    x_hbm, qkv_hbm, out_hbm, next_qkv_hbm, next_out_hbm,
    *refs,
):
    y_refs, refs = (refs[:2], refs[2:]) if chips else (refs[:1], refs[1:])
    next_qkv_ref, next_out_ref, x_ref, qkv_ref, out_ref, packed_ref, heads_ref, sems = refs
    width = x_ref.shape[1]
    fetch_x = pltpu.make_async_copy(x_hbm, x_ref, sems.at[0])
    fetch_x.start()
    parts = []
    for part in range(3):
        columns = slice(part * width, (part + 1) * width)
        copy = pltpu.make_async_copy(
            qkv_hbm.at[:, columns], qkv_ref.at[:, columns], sems.at[part + 1]
        )
        copy.start()
        parts.append((columns, copy))
    fetch_out = pltpu.make_async_copy(out_hbm, out_ref, sems.at[4])
    fetch_out.start()
    fetch_next_qkv = pltpu.make_async_copy(next_qkv_hbm, next_qkv_ref, sems.at[5])
    fetch_next_qkv.start()
    fetch_next_out = pltpu.make_async_copy(next_out_hbm, next_out_ref, sems.at[6])
    fetch_next_out.start()
    fetch_x.wait()
    x = blocks_by_distance(x_ref, chips) if chips else x_ref[...]
    normed = norm_rows(x.astype(F32))
    for columns, copy in parts:
        copy.wait()
        packed_ref[:, columns] = dot(normed, qkv_ref[:, columns]).astype(BF16)
    attend_rows(packed_ref, heads_ref, 0)
    fetch_out.wait()
    y = (x.astype(F32) + dot(heads_ref[...], out_ref[...])).astype(BF16)
    if chips:
        y_refs[0][...], y_refs[1][...] = split_near(y, chips)
    else:
        y_refs[0][...] = y
    fetch_next_qkv.wait()
    fetch_next_out.wait()


def spatial_layer(rows, w_qkv, w_out, next_qkv, next_out, chips):
    count, width = rows.shape
    halves = 2 if chips else 1
    return pl.pallas_call(
        functools.partial(spatial_kernel, chips),
        out_shape=[jax.ShapeDtypeStruct((count // halves, width), BF16)] * halves
        + [
            jax.ShapeDtypeStruct(next_qkv.shape, BF16),
            jax.ShapeDtypeStruct(next_out.shape, BF16),
        ],
        in_specs=[pl.BlockSpec(memory_space=pltpu.HBM)] * 5,
        out_specs=vmem(halves + 2),
        scratch_shapes=[
            pltpu.VMEM(rows.shape, BF16),
            pltpu.VMEM(w_qkv.shape, BF16),
            pltpu.VMEM(w_out.shape, BF16),
            pltpu.VMEM((count, 3 * width), BF16),
            pltpu.VMEM((count, width), BF16),
            pltpu.SemaphoreType.DMA((7,)),
        ],
        compiler_params=params(count),
    )(*in_hbm(rows, w_qkv, w_out, next_qkv, next_out))


def temporal_kernel(stride, x_ref, qkv_ref, out_ref, y_ref, packed_ref, heads_ref):
    normed = norm_rows(x_ref[...].astype(F32))
    packed_ref[...] = dot(normed, qkv_ref[...]).astype(BF16)
    attend_rows(packed_ref, heads_ref, stride)
    y_ref[...] = (x_ref[...].astype(F32) + dot(heads_ref[...], out_ref[...])).astype(BF16)


def temporal_layer(rows, w_qkv, w_out, stride):
    count, width = rows.shape
    return pl.pallas_call(
        functools.partial(temporal_kernel, stride),
        out_shape=jax.ShapeDtypeStruct((count, width), BF16),
        in_specs=vmem(3),
        out_specs=vmem(1)[0],
        scratch_shapes=[
            pltpu.VMEM((count, 3 * width), BF16),
            pltpu.VMEM((count, width), BF16),
        ],
        compiler_params=params(count),
    )(rows, w_qkv, w_out)


def by_patch_group(values, size):
    groups = size // SUBLANES
    frames = values.shape[0] // size
    return jnp.concatenate(
        [
            values[frame * size + group * SUBLANES : frame * size + (group + 1) * SUBLANES]
            for group in range(groups)
            for frame in range(frames)
        ],
        axis=0,
    )


def by_frame(values, size):
    groups = size // SUBLANES
    frames = values.shape[0] // size
    return jnp.concatenate(
        [
            values[(group * frames + frame) * SUBLANES : (group * frames + frame + 1) * SUBLANES]
            for frame in range(frames)
            for group in range(groups)
        ],
        axis=0,
    )


def normed_groups(x, size):
    x = x.astype(F32)
    center = x - jnp.mean(x, axis=-1, keepdims=True)
    spread = jnp.mean(center * center, axis=-1, keepdims=True)
    return by_patch_group(center * lax.rsqrt(spread + 1e-05), size).astype(BF16)


def project_kernel(size, x_ref, qkv_ref, packed_ref):
    packed_ref[...] = dot(normed_groups(x_ref[...], size), qkv_ref[...]).astype(BF16)


def project_own(rows, w_qkv, size):
    count, width = rows.shape
    return pl.pallas_call(
        functools.partial(project_kernel, size),
        out_shape=jax.ShapeDtypeStruct((count, w_qkv.shape[1]), BF16),
        in_specs=vmem(2),
        out_specs=vmem(1)[0],
        compiler_params=params(count),
        cost_estimate=pl.CostEstimate(
            flops=2 * count * width * w_qkv.shape[1],
            bytes_accessed=2 * (rows.size + w_qkv.size + count * w_qkv.shape[1]),
            transcendentals=0,
        ),
    )(rows, w_qkv)


def shared_kernel(size, chips, x_ref, packed_ref, other_ref, qkv_ref, out_ref, keep_ref, send_ref, heads_ref):
    count, width = x_ref.shape
    pair = 2 * (width // HEADS)
    other = dot(normed_groups(other_ref[...], size), qkv_ref[:, width:]).astype(BF16)
    groups = size // SUBLANES
    block = count // groups
    ones = pair_ones(2 * block, pair // 2)
    same = same_modulo(block, 2 * block, SUBLANES)
    for at in range(0, width, pair):
        for group in range(groups):
            here = slice(group * block, (group + 1) * block)
            key, value = (
                jnp.concatenate(
                    [packed_ref[here, skip + at : skip + at + pair],
                     other[here, skip - width + at : skip - width + at + pair]],
                    axis=0,
                )
                for skip in (width, 2 * width)
            )
            heads_ref[here, at : at + pair] = attend_pair(
                packed_ref[here, at : at + pair], key, value, ones, same
            )
    merged = by_frame(dot(heads_ref[...], out_ref[...]), size)
    y = (x_ref[...].astype(F32) + merged).astype(BF16)
    keep_ref[...], send_ref[...] = split_near(y, chips)


def shared_layer(rows, packed, other, w_qkv, w_out, size, chips):
    count, width = rows.shape
    return pl.pallas_call(
        functools.partial(shared_kernel, size, chips),
        out_shape=[jax.ShapeDtypeStruct((count // 2, width), BF16)] * 2,
        in_specs=vmem(5),
        out_specs=vmem(2),
        scratch_shapes=[pltpu.VMEM((count, width), BF16)],
        compiler_params=params(count),
    )(rows, packed, other, w_qkv, w_out)


def mlp_block(x, up_ref, down_ref):
    normed = norm_rows(x.astype(F32))
    u = dot(normed, up_ref[...])
    half = 0.5 * u
    bend = jnp.tanh(u * (0.7978845608028654 + 0.035677408136300125 * (u * u)))
    hidden = (half + half * bend).astype(BF16)
    return (x.astype(F32) + dot(hidden, down_ref[...])).astype(BF16)


def mlp_kernel(x_ref, up_ref, down_ref, y_ref):
    rows = x_ref.shape[0]
    block = min(rows, LANES)

    @pl.loop(0, rows // block)
    def _(index):
        here = pl.ds(pl.multiple_of(index * block, block), block)
        y_ref[here, :] = mlp_block(x_ref[here, :], up_ref, down_ref)


def mlp_layer(rows, w_up, w_down):
    return pl.pallas_call(
        mlp_kernel,
        out_shape=jax.ShapeDtypeStruct(rows.shape, BF16),
        in_specs=vmem(3),
        out_specs=vmem(1)[0],
        compiler_params=params(rows.shape[0]),
    )(rows, w_up, w_down)


def mlp_parts_kernel(chips, *refs):
    part_refs, (up_ref, down_ref, y_ref) = refs[:-3], refs[-3:]
    y = mlp_block(jnp.concatenate([each[...] for each in part_refs], axis=0), up_ref, down_ref)
    size = y.shape[0] // chips
    mine = lax.axis_index("seq") // 2
    for distance in range(chips):
        here = pl.ds(pl.multiple_of((mine ^ distance) * size, size), size)
        y_ref[here, :] = y[distance * size : (distance + 1) * size]


def mlp_parts_layer(parts, w_up, w_down, chips):
    count = sum(each.shape[0] for each in parts)
    return pl.pallas_call(
        functools.partial(mlp_parts_kernel, chips),
        out_shape=jax.ShapeDtypeStruct((count, parts[0].shape[1]), BF16),
        in_specs=vmem(len(parts) + 2),
        out_specs=vmem(1)[0],
        compiler_params=params(count),
    )(*parts, w_up, w_down)


def swap(rows, distance):
    pairs = [(at, at ^ distance) for at in range(lax.axis_size("seq"))]
    return lax.ppermute(rows, "seq", pairs)


def exchange(keep, send, far):
    got = swap(send, 2)
    size = keep.shape[0] // far

    def both(at):
        here = slice(at * size, (at + 1) * size)
        return jnp.concatenate([keep[here], got[here]], axis=0)

    arrived = {at: swap(both(at), 4 * at) for at in range(far - 1, 0, -1)}
    return [both(0)] + [arrived[at] for at in range(1, far)]


def by_permutes(tokens, spatial_qkv, spatial_out, temporal_qkv, temporal_out, mlp_up, mlp_down):
    devices = lax.axis_size("seq")
    chips, far = devices // 2, devices // 4
    size = tokens.shape[0] // chips
    keep, send, next_qkv, next_out = spatial_layer(
        tokens, spatial_qkv, spatial_out, temporal_qkv, temporal_out, chips
    )
    own = jnp.concatenate(exchange(keep, send, far), axis=0)
    other = swap(own, 1)
    packed = project_own(own, next_qkv, size)
    keep, send = shared_layer(own, packed, other, next_qkv, next_out, size, chips)
    return mlp_parts_layer(exchange(keep, send, far), mlp_up, mlp_down, chips)


def by_all_to_all(clip_tokens, spatial_qkv, spatial_out, temporal_qkv, temporal_out, mlp_up, mlp_down):
    frame_count, patches, width = clip_tokens.shape
    devices = lax.axis_size("seq")
    share = patches // devices
    frames = frame_count * devices
    mixed = []
    for index in range(frame_count):
        rows, next_qkv, next_out = spatial_layer(
            clip_tokens[index], spatial_qkv, spatial_out, temporal_qkv, temporal_out, 0
        )
        mixed.append(rows)
    blocks = jnp.stack(mixed).reshape(frame_count, devices, share, width)
    arrived = lax.all_to_all(blocks, "seq", split_axis=1, concat_axis=0, tiled=True)
    tokens = arrived.reshape(frames * share, width)
    after_time = temporal_layer(tokens, next_qkv, next_out, share)
    returned = after_time.reshape(frames, 1, share, width)
    back = lax.all_to_all(returned, "seq", split_axis=0, concat_axis=1, tiled=True)
    return mlp_layer(back.reshape(frame_count * patches, width), mlp_up, mlp_down)


def local(clip_tokens, *weights):
    frame_count, patches, width = clip_tokens.shape
    devices = lax.axis_size("seq")
    if (
        frame_count == 1
        and devices in (4, 8, 16)
        and patches % (SUBLANES * devices) == 0
        and patches <= LANES
    ):
        result = by_permutes(clip_tokens.reshape(patches, width), *weights)
    else:
        result = by_all_to_all(clip_tokens, *weights)
    return result.reshape(frame_count, patches, width)


def solution(mesh):
    in_specs = (P(("groups", "seq"), None, None), P(), P(), P(), P(), P(), P())
    out_specs = P(("groups", "seq"), None, None)
    return jax.shard_map(local, mesh=mesh, in_specs=in_specs, out_specs=out_specs, check_vma=False)
```

time: 32 us -> 33.6 us (1.050)
  blocking collectives: 25.8 us -> 0 us
  starting transfers between devices: 0 us -> 13.8 us
  waiting for transfers between devices: 0 us -> 13.7 us
    all_to_all x2 -> x0, blocking collectives: 25.8 us -> none  [the longest x1 15.3 us: local(): lax.all_to_all(blocks, 'seq', split_axis=1, concat_axis=0, tiled=True)]
    ppermute x0 -> x9, starting transfers between devices: none -> 13.8 us  [swap(): return lax.ppermute(rows, 'seq', pairs)]
    ppermute x0 -> x9, waiting for transfers between devices: none -> 13.7 us  [swap(): return lax.ppermute(rows, 'seq', pairs)]
    pallas_call x3 -> x4, Pallas kernels: 5.95 us -> 5.86 us  [the longest x1 2.49 us: spatial_layer(): pl.pallas_call(functools.partial(spatial_kernel, chips), out_shape=[jax.S...]
  transfers between devices with their start and end apart: 0 -> 9, of which waited for: 0 -> 7; matrix products, arithmetic and copies ran while one was open for 0% -> 0% of each run, Pallas kernels for 0% -> 2%
where the time goes in v3:
time: 33.6 us; the launch traced here: 33.5 us
  starting transfers between devices  13.8 us (41%)
  waiting for transfers between devices  13.7 us (41%)
  Pallas kernels  5.86 us (17%)
    ppermute x9, starting transfers between devices, swap(): return lax.ppermute(rows, 'seq', pairs)  13.8 us
    ppermute x9, waiting for transfers between devices, swap(): return lax.ppermute(rows, 'seq', pairs)  13.7 us
    pallas_call x1, Pallas kernels, spatial_layer(): pl.pallas_call(functools.partial(spatial_kernel, chips), out_shape=[jax.S...  2.49 us
    pallas_call x1, Pallas kernels, mlp_parts_layer(): pl.pallas_call(functools.partial(mlp_parts_kernel, chips), out_shape=jax....  1.68 us
    pallas_call x1, Pallas kernels, shared_layer(): pl.pallas_call(functools.partial(shared_kernel, size, chips), out_shape=[...  1.16 us
  transfers between devices with their start and end apart: 9, of which 7 were waited for; matrix products, arithmetic and copies ran while one was open for 0% of the time, Pallas kernels for 2%

profile of v3, /device:TPU:0, one launch (start us, length us, event | category | flops | bytes accessed | tf_op | source)
XLA Modules:
  0.0 33.5 jit_solution(11588564460546954203)
XLA Ops:
  0.0 2.5 %shard_map.73 = (bf16[64,512]{1,0:T(8,128)(2,1)S(1)}, bf16[64,512]{1,0:T(8,128)(2,1)S(1)}, bf16[512,1536]{1,0:T(8,128)(2,1)S(1)}, bf16[512,512]{1,0:T(8,128)(2,1)S(1)}) custom-call(bf16[128,512]{1,0:T(8,128)(2,1)} %bitcast.2, bf16[512,1536]{1,0:T(8,128)(2,1)} %qkv_hbm.1, bf16[512,512]{1,0:T(8,128)(2,1)} %out_hbm.1, bf16[512,1536]{1,0:T(8,128)(2,1)} %next_qkv_hbm.1, ...), custom_call_target="tpu_custom_call" | custom-call | tf_op jit(solution)/shard_map/pallas_call | solution.py:168
  2.5 3.0 %collective-permute-start = (bf16[64,512]{1,0:T(8,128)(2,1)S(1)}, bf16[64,512]{1,0:T(8,128)(2,1)S(1)}, u32[]{:S(2)}, u32[]{:S(2)}) collective-permute-start(bf16[64,512]{1,0:T(8,128)(2,1)S(1)} %get-tuple-element.12), channel_id=1, source_target_pairs={{0,2},{1,3},{2,0},{3,1},{4,6},{5,7},{6,4},{7,5},{8,10},{9,11},{10,... | collective-permute-start | bytes 196616 | tf_op jit(solution)/shard_map/ppermute | solution.py:355
  5.5 2.2 %collective-permute-done = bf16[64,512]{1,0:T(8,128)(2,1)S(1)} collective-permute-done((bf16[64,512]{1,0:T(8,128)(2,1)S(1)}, bf16[64,512]{1,0:T(8,128)(2,1)S(1)}, u32[]{:S(2)}, u32[]{:S(2)}) %collective-permute-start) | collective-permute-done | bytes 65568 | tf_op jit(solution)/shard_map/ppermute | solution.py:355
  7.8 2.1 %collective-permute-start.1 = (bf16[32,512]{1,0:T(8,128)(2,1)S(1)}, bf16[32,512]{1,0:T(8,128)(2,1)S(1)}, u32[]{:S(2)}, u32[]{:S(2)}) collective-permute-start(bf16[32,512]{1,0:T(8,128)(2,1)S(1)} %pad_maximum_fusion), channel_id=1, source_target_pairs={{0,4},{1,5},{2,6},{3,7},{4,0},{5,1},{6,2},{7,3},{8,12},{9,13},{10,... | collective-permute-start | bytes 98312 | tf_op jit(solution)/shard_map/ppermute | solution.py:355
  9.9 2.6 %collective-permute-start.2 = (bf16[32,512]{1,0:T(8,128)(2,1)S(1)}, bf16[32,512]{1,0:T(8,128)(2,1)S(1)}, u32[]{:S(2)}, u32[]{:S(2)}) collective-permute-start(bf16[32,512]{1,0:T(8,128)(2,1)S(1)} %pad_maximum_fusion.1), channel_id=1, source_target_pairs={{0,8},{1,9},{2,10},{3,11},{4,12},{5,13},{6,14},{7,15},{8,0},{9,1},... | collective-permute-start | bytes 98312 | tf_op jit(solution)/shard_map/ppermute | solution.py:355
  12.5 0.0 collective-permute-start.3
  12.5 0.0 collective-permute-done.1
  12.5 2.4 %collective-permute-done.2 = bf16[32,512]{1,0:T(8,128)(2,1)S(1)} collective-permute-done((bf16[32,512]{1,0:T(8,128)(2,1)S(1)}, bf16[32,512]{1,0:T(8,128)(2,1)S(1)}, u32[]{:S(2)}, u32[]{:S(2)}) %collective-permute-start.2) | collective-permute-done | bytes 32800 | tf_op jit(solution)/shard_map/ppermute | solution.py:355
  15.0 3.2 %collective-permute-done.3 = bf16[32,512]{1,0:T(8,128)(2,1)S(1)} collective-permute-done((bf16[32,512]{1,0:T(8,128)(2,1)S(1)}, bf16[32,512]{1,0:T(8,128)(2,1)S(1)}, u32[]{:S(2)}, u32[]{:S(2)}) %collective-permute-start.3) | collective-permute-done | bytes 32800 | tf_op jit(solution)/shard_map/ppermute | solution.py:355
  18.2 0.0 collective-permute-start.4
  18.2 0.0 copy-start.1
  18.3 0.5 %shard_map.74.packed_ref = bf16[128,1536]{1,0:T(8,128)(2,1)S(1)} custom-call(bf16[128,512]{1,0:T(8,128)(2,1)S(1)} %constant_dynamic-update-slice_fusion.x_ref, bf16[512,1536]{1,0:T(8,128)(2,1)S(1)} %get-tuple-element.13.qkv_ref), custom_call_target="tpu_custom_call" | custom-call | flops 201326592 | bytes 2097152 | tf_op jit(solution)/shard_map/pallas_call | solution.py:250
  18.8 0.8 %collective-permute-done.4.other_ref = bf16[128,512]{1,0:T(8,128)(2,1)S(1)} collective-permute-done((bf16[128,512]{1,0:T(8,128)(2,1)S(1)}, bf16[128,512]{1,0:T(8,128)(2,1)S(1)}, u32[]{:S(2)}, u32[]{:S(2)}) %collective-permute-start.4) | collective-permute-done | bytes 131104 | tf_op jit(solution)/shard_map/ppermute | solution.py:355
  19.6 0.0 copy-start
  19.6 1.2 %shard_map.75 = (bf16[64,512]{1,0:T(8,128)(2,1)S(1)}, bf16[64,512]{1,0:T(8,128)(2,1)S(1)}) custom-call(bf16[128,512]{1,0:T(8,128)(2,1)S(1)} %constant_dynamic-update-slice_fusion.x_ref, bf16[128,1536]{1,0:T(8,128)(2,1)S(1)} %shard_map.74.packed_ref, bf16[128,512]{1,0:T(8,128)(2,1)S(1)} %collective-permute-done.4.other_ref, ...), custom_call_target="tpu_custom_call" | custom-call | tf_op jit(solution)/shard_map/pallas_call | solution.py:293
  20.8 1.6 %collective-permute-start.5 = (bf16[64,512]{1,0:T(8,128)(2,1)S(1)}, bf16[64,512]{1,0:T(8,128)(2,1)S(1)}, u32[]{:S(2)}, u32[]{:S(2)}) collective-permute-start(bf16[64,512]{1,0:T(8,128)(2,1)S(1)} %get-tuple-element.16), channel_id=1, source_target_pairs={{0,2},{1,3},{2,0},{3,1},{4,6},{5,7},{6,4},{7,5},{8,10},{9,11},{10,... | collective-permute-start | bytes 196616 | tf_op jit(solution)/shard_map/ppermute | solution.py:355
  22.3 2.7 %collective-permute-done.5 = bf16[64,512]{1,0:T(8,128)(2,1)S(1)} collective-permute-done((bf16[64,512]{1,0:T(8,128)(2,1)S(1)}, bf16[64,512]{1,0:T(8,128)(2,1)S(1)}, u32[]{:S(2)}, u32[]{:S(2)}) %collective-permute-start.5) | collective-permute-done | bytes 65568 | tf_op jit(solution)/shard_map/ppermute | solution.py:355
  25.1 0.1 collective-permute-start.6
  25.2 0.9 %collective-permute-start.7 = (bf16[32,512]{1,0:T(8,128)(2,1)S(1)}, bf16[32,512]{1,0:T(8,128)(2,1)S(1)}, u32[]{:S(2)}, u32[]{:S(2)}) collective-permute-start(bf16[32,512]{1,0:T(8,128)(2,1)S(1)} %pad_maximum_fusion.5), channel_id=1, source_target_pairs={{0,8},{1,9},{2,10},{3,11},{4,12},{5,13},{6,14},{7,15},{8,0},{9,1},... | collective-permute-start | bytes 98312 | tf_op jit(solution)/shard_map/ppermute | solution.py:355
  26.1 3.5 %collective-permute-start.8 = (bf16[32,512]{1,0:T(8,128)(2,1)S(1)}, bf16[32,512]{1,0:T(8,128)(2,1)S(1)}, u32[]{:S(2)}, u32[]{:S(2)}) collective-permute-start(bf16[32,512]{1,0:T(8,128)(2,1)S(1)} %pad_maximum_fusion.6), channel_id=1, source_target_pairs={{0,12},{1,13},{2,14},{3,15},{4,8},{5,9},{6,10},{7,11},{8,4},{9,5},... | collective-permute-start | bytes 98312 | tf_op jit(solution)/shard_map/ppermute | solution.py:355
  29.6 0.0 collective-permute-done.6.refs_1_
  29.6 0.5 %collective-permute-done.7.refs_2_ = bf16[32,512]{1,0:T(8,128)(2,1)S(1)} collective-permute-done((bf16[32,512]{1,0:T(8,128)(2,1)S(1)}, bf16[32,512]{1,0:T(8,128)(2,1)S(1)}, u32[]{:S(2)}, u32[]{:S(2)}) %collective-permute-start.7) | collective-permute-done | bytes 32800 | tf_op jit(solution)/shard_map/ppermute | solution.py:355
  30.1 1.7 %collective-permute-done.8.refs_3_ = bf16[32,512]{1,0:T(8,128)(2,1)S(1)} collective-permute-done((bf16[32,512]{1,0:T(8,128)(2,1)S(1)}, bf16[32,512]{1,0:T(8,128)(2,1)S(1)}, u32[]{:S(2)}, u32[]{:S(2)}) %collective-permute-start.8) | collective-permute-done | bytes 32800 | tf_op jit(solution)/shard_map/ppermute | solution.py:355
  31.8 0.0 copy-done.1
  31.8 0.0 copy-done
  31.8 1.7 %shard_map.76 = bf16[128,512]{1,0:T(8,128)(2,1)} custom-call(bf16[32,512]{1,0:T(8,128)(2,1)S(1)} %pad_maximum_fusion.3.refs_0_, bf16[32,512]{1,0:T(8,128)(2,1)S(1)} %collective-permute-done.6.refs_1_, bf16[32,512]{1,0:T(8,128)(2,1)S(1)} %collective-permute-done.7.refs_2_, bf16[32,512]{1,0:T(8,128)(2,1)S(1)} %collective-permute-done.8.refs_3_, ...), custom_call_target="tpu_custom_call" | custom-call | tf_op jit(solution)/shard_map/pallas_call | solution.py:344
  (14 shorter events, 0.1 us)
Async XLA Ops:
  2.5 5.3 %collective-permute-start = (bf16[64,512]{1,0:T(8,128)(2,1)S(1)}, bf16[64,512]{1,0:T(8,128)(2,1)S(1)}, u32[]{:S(2)}, u32[]{:S(2)}) collective-permute-start(bf16[64,512]{1,0:T(8,128)(2,1)S(1)} %get-tuple-element.12), channel_id=1, source_target_pairs={{0,2},{1,3},{2,0},{3,1},{4,6},{5,7},{6,4},{7,5},{8,10},{9,11},{10,... | collective-permute-start | bytes 196616 | tf_op jit(solution)/shard_map/ppermute | solution.py:355
  7.8 4.7 %collective-permute-start.1 = (bf16[32,512]{1,0:T(8,128)(2,1)S(1)}, bf16[32,512]{1,0:T(8,128)(2,1)S(1)}, u32[]{:S(2)}, u32[]{:S(2)}) collective-permute-start(bf16[32,512]{1,0:T(8,128)(2,1)S(1)} %pad_maximum_fusion), channel_id=1, source_target_pairs={{0,4},{1,5},{2,6},{3,7},{4,0},{5,1},{6,2},{7,3},{8,12},{9,13},{10,... | collective-permute-start | bytes 98312 | tf_op jit(solution)/shard_map/ppermute | solution.py:355
  9.9 5.1 %collective-permute-start.2 = (bf16[32,512]{1,0:T(8,128)(2,1)S(1)}, bf16[32,512]{1,0:T(8,128)(2,1)S(1)}, u32[]{:S(2)}, u32[]{:S(2)}) collective-permute-start(bf16[32,512]{1,0:T(8,128)(2,1)S(1)} %pad_maximum_fusion.1), channel_id=1, source_target_pairs={{0,8},{1,9},{2,10},{3,11},{4,12},{5,13},{6,14},{7,15},{8,0},{9,1},... | collective-permute-start | bytes 98312 | tf_op jit(solution)/shard_map/ppermute | solution.py:355
  12.5 5.7 %collective-permute-start.3 = (bf16[32,512]{1,0:T(8,128)(2,1)S(1)}, bf16[32,512]{1,0:T(8,128)(2,1)S(1)}, u32[]{:S(2)}, u32[]{:S(2)}) collective-permute-start(bf16[32,512]{1,0:T(8,128)(2,1)S(1)} %pad_maximum_fusion.2), channel_id=1, source_target_pairs={{0,12},{1,13},{2,14},{3,15},{4,8},{5,9},{6,10},{7,11},{8,4},{9,5},... | collective-permute-start | bytes 98312 | tf_op jit(solution)/shard_map/ppermute | solution.py:355
  18.2 1.3 %collective-permute-start.4 = (bf16[128,512]{1,0:T(8,128)(2,1)S(1)}, bf16[128,512]{1,0:T(8,128)(2,1)S(1)}, u32[]{:S(2)}, u32[]{:S(2)}) collective-permute-start(bf16[128,512]{1,0:T(8,128)(2,1)S(1)} %constant_dynamic-update-slice_fusion.x_ref), channel_id=1, source_target_pairs={{0,1},{1,0},{2,3},{3,2},{4,5},{5,4},{6,7},{7,6},{8,9},{9,8},{10,11... | collective-permute-start | bytes 393224 | tf_op jit(solution)/shard_map/ppermute | solution.py:355
  18.2 13.6 %copy-start.1 = (bf16[2048,512]{1,0:T(8,128)(2,1)S(1)}, bf16[2048,512]{1,0:T(8,128)(2,1)}, u32[]{:S(2)}) copy-start(bf16[2048,512]{1,0:T(8,128)(2,1)} %refs_5_.1) | copy-start | bytes 6291460
  19.6 12.2 %copy-start = (bf16[512,2048]{1,0:T(8,128)(2,1)S(1)}, bf16[512,2048]{1,0:T(8,128)(2,1)}, u32[]{:S(2)}) copy-start(bf16[512,2048]{1,0:T(8,128)(2,1)} %refs_4_.1) | copy-start | bytes 6291460
  20.8 4.3 %collective-permute-start.5 = (bf16[64,512]{1,0:T(8,128)(2,1)S(1)}, bf16[64,512]{1,0:T(8,128)(2,1)S(1)}, u32[]{:S(2)}, u32[]{:S(2)}) collective-permute-start(bf16[64,512]{1,0:T(8,128)(2,1)S(1)} %get-tuple-element.16), channel_id=1, source_target_pairs={{0,2},{1,3},{2,0},{3,1},{4,6},{5,7},{6,4},{7,5},{8,10},{9,11},{10,... | collective-permute-start | bytes 196616 | tf_op jit(solution)/shard_map/ppermute | solution.py:355
  25.1 4.5 %collective-permute-start.6 = (bf16[32,512]{1,0:T(8,128)(2,1)S(1)}, bf16[32,512]{1,0:T(8,128)(2,1)S(1)}, u32[]{:S(2)}, u32[]{:S(2)}) collective-permute-start(bf16[32,512]{1,0:T(8,128)(2,1)S(1)} %pad_maximum_fusion.4), channel_id=1, source_target_pairs={{0,4},{1,5},{2,6},{3,7},{4,0},{5,1},{6,2},{7,3},{8,12},{9,13},{10,... | collective-permute-start | bytes 98312 | tf_op jit(solution)/shard_map/ppermute | solution.py:355
  25.2 4.9 %collective-permute-start.7 = (bf16[32,512]{1,0:T(8,128)(2,1)S(1)}, bf16[32,512]{1,0:T(8,128)(2,1)S(1)}, u32[]{:S(2)}, u32[]{:S(2)}) collective-permute-start(bf16[32,512]{1,0:T(8,128)(2,1)S(1)} %pad_maximum_fusion.5), channel_id=1, source_target_pairs={{0,8},{1,9},{2,10},{3,11},{4,12},{5,13},{6,14},{7,15},{8,0},{9,1},... | collective-permute-start | bytes 98312 | tf_op jit(solution)/shard_map/ppermute | solution.py:355
  26.1 5.7 %collective-permute-start.8 = (bf16[32,512]{1,0:T(8,128)(2,1)S(1)}, bf16[32,512]{1,0:T(8,128)(2,1)S(1)}, u32[]{:S(2)}, u32[]{:S(2)}) collective-permute-start(bf16[32,512]{1,0:T(8,128)(2,1)S(1)} %pad_maximum_fusion.6), channel_id=1, source_target_pairs={{0,12},{1,13},{2,14},{3,15},{4,8},{5,9},{6,10},{7,11},{8,4},{9,5},... | collective-permute-start | bytes 98312 | tf_op jit(solution)/shard_map/ppermute | solution.py:355

commit v4 on v2

v4 whole, which is shorter than its diff:
```python
import functools

import jax
import jax.numpy as jnp
from jax import lax
from jax.experimental import pallas as pl
from jax.experimental.pallas import tpu as pltpu
from jax.sharding import PartitionSpec as P

HEADS = 8
LANES = 128
BF16 = jnp.bfloat16
F32 = jnp.float32
MIB = 1024 * 1024


def vmem_limit(rows):
    return 10 * MIB + rows * 32 * 1024


def params(rows):
    return pltpu.CompilerParams(vmem_limit_bytes=vmem_limit(rows))


def in_hbm(*arrays):
    return tuple(pltpu.with_memory_space_constraint(each, pltpu.HBM) for each in arrays)


def vmem(count):
    return [pl.BlockSpec(memory_space=pltpu.VMEM)] * count


def norm_rows(values):
    center = values - jnp.mean(values, axis=-1, keepdims=True)
    spread = jnp.mean(center * center, axis=-1, keepdims=True)
    return (center * lax.rsqrt(spread + 1e-05)).astype(BF16)


def dot(left, right):
    return jnp.dot(left, right, preferred_element_type=F32)


def pair_ones(keys, head):
    low = lax.broadcasted_iota(jnp.int32, (keys, 2 * head), 1) < head
    return jnp.concatenate(
        [jnp.where(low, 1.0, 0.0), jnp.where(low, 0.0, 1.0)], axis=0
    ).astype(BF16)


def attend_heads(query, key, value, ones, same):
    block, width = query.shape
    head = width // HEADS
    pair = 2 * head
    scale = head ** (-0.5) * 1.4426950408889634
    low_q = lax.broadcasted_iota(jnp.int32, (block, pair), 1) < head
    low_v = lax.broadcasted_iota(jnp.int32, (value.shape[0], pair), 1) < head

    def split(part, low):
        zero = jnp.zeros_like(part)
        return jnp.concatenate([jnp.where(low, part, zero), jnp.where(low, zero, part)], axis=0)

    heads = []
    for at in range(0, width, pair):
        here = slice(at, at + pair)
        scores = lax.dot_general(
            split(query[:, here], low_q), key[:, here], (((1,), (1,)), ((), ())),
            preferred_element_type=F32,
        )
        if same is not None:
            scores = jnp.where(same, scores, -jnp.inf)
        top = jnp.max(scores, axis=-1, keepdims=True)
        raised = jnp.exp2((scores - top) * scale).astype(BF16)
        side = jnp.concatenate([raised[:block], raised[block:]], axis=1)
        total = dot(side, jnp.concatenate([split(value[:, here], low_v), ones], axis=1))
        heads.append((total[:, :pair] / total[:, pair:]).astype(BF16))
    return jnp.concatenate(heads, axis=1)


def same_modulo(queries, keys, stride, start=0):
    query_at = start + lax.broadcasted_iota(jnp.int32, (2 * queries, keys), 0)
    key_at = lax.broadcasted_iota(jnp.int32, (2 * queries, keys), 1)
    return lax.rem(query_at, stride) == lax.rem(key_at, stride)


def attend_and_project(packed, w_out, x, y_ref, heads_ref, stride):
    rows, width = y_ref.shape
    pair = 2 * (width // HEADS)
    block = min(rows, LANES)
    ones = pair_ones(rows, pair // 2)
    keys, values = packed[:, width : 2 * width], packed[:, 2 * width :]
    if rows == block:
        same = same_modulo(block, rows, stride) if stride else None
        heads = attend_heads(packed[:, :width], keys, values, ones, same)
        y_ref[...] = (x + dot(heads, w_out[...])).astype(BF16)
    else:

        @pl.loop(0, rows // block)
        def _(index):
            start = pl.multiple_of(index * block, block)
            here = pl.ds(start, block)
            same = same_modulo(block, rows, stride, start) if stride else None
            heads_ref[here, :] = attend_heads(packed[here, :width], keys, values, ones, same)

        y_ref[...] = (x + dot(heads_ref[...], w_out[...])).astype(BF16)


def spatial_kernel(
    x_hbm, qkv_hbm, out_hbm, next_qkv_hbm, next_out_hbm,
    y_ref, next_qkv_ref, next_out_ref,
    x_ref, qkv_ref, out_ref, packed_ref, heads_ref, sems,
):
    width = x_ref.shape[1]

    def fetch(source, target, at):
        copy = pltpu.make_async_copy(source, target, sems.at[at])
        copy.start()
        return copy

    x_copy = fetch(x_hbm, x_ref, 0)
    copies = []
    for block in range(3):
        columns = slice(block * width, (block + 1) * width)
        copies.append(fetch(qkv_hbm.at[:, columns], qkv_ref.at[:, columns], 1 + block))
    out_copy = fetch(out_hbm, out_ref, 4)
    next_copies = [
        fetch(next_qkv_hbm, next_qkv_ref, 5), fetch(next_out_hbm, next_out_ref, 6)
    ]
    x_copy.wait()
    x = x_ref[...].astype(F32)
    normed = norm_rows(x)
    for block, copy in enumerate(copies):
        columns = slice(block * width, (block + 1) * width)
        copy.wait()
        packed_ref[:, columns] = dot(normed, qkv_ref[:, columns]).astype(BF16)
    out_copy.wait()
    attend_and_project(packed_ref, out_ref, x, y_ref, heads_ref, 0)
    for copy in next_copies:
        copy.wait()


def spatial_layer(rows, w_qkv, w_out, next_qkv, next_out):
    count, width = rows.shape
    return pl.pallas_call(
        spatial_kernel,
        out_shape=[
            jax.ShapeDtypeStruct((count, width), BF16),
            jax.ShapeDtypeStruct(next_qkv.shape, BF16),
            jax.ShapeDtypeStruct(next_out.shape, BF16),
        ],
        in_specs=[pl.BlockSpec(memory_space=pltpu.HBM)] * 5,
        out_specs=vmem(3),
        scratch_shapes=[
            pltpu.VMEM(rows.shape, BF16),
            pltpu.VMEM(w_qkv.shape, BF16),
            pltpu.VMEM(w_out.shape, BF16),
            pltpu.VMEM((count, 3 * width), BF16),
            pltpu.VMEM((count, width), BF16),
            pltpu.SemaphoreType.DMA((7,)),
        ],
        compiler_params=params(count),
    )(*in_hbm(rows, w_qkv, w_out, next_qkv, next_out))


def temporal_kernel(stride, x_ref, qkv_ref, out_ref, y_ref, packed_ref, heads_ref):
    x = x_ref[...].astype(F32)
    packed = dot(norm_rows(x), qkv_ref[...]).astype(BF16)
    if x.shape[0] > LANES:
        packed_ref[...] = packed
        packed = packed_ref
    attend_and_project(packed, out_ref, x, y_ref, heads_ref, stride)


def temporal_layer(rows, w_qkv, w_out, stride):
    count, width = rows.shape
    return pl.pallas_call(
        functools.partial(temporal_kernel, stride),
        out_shape=jax.ShapeDtypeStruct((count, width), BF16),
        in_specs=vmem(3),
        out_specs=vmem(1)[0],
        scratch_shapes=[
            pltpu.VMEM((count, 3 * width), BF16),
            pltpu.VMEM((count, width), BF16),
        ],
        compiler_params=params(count),
    )(rows, w_qkv, w_out)


def mlp_block(x, up_ref, down_ref):
    normed = norm_rows(x.astype(F32))
    u = dot(normed, up_ref[...])
    half = 0.5 * u
    bend = jnp.tanh(u * (0.7978845608028654 + 0.035677408136300125 * (u * u)))
    hidden = (half + half * bend).astype(BF16)
    return (x.astype(F32) + dot(hidden, down_ref[...])).astype(BF16)


def mlp_kernel(x_ref, up_ref, down_ref, y_ref):
    rows = x_ref.shape[0]
    block = min(rows, LANES)

    @pl.loop(0, rows // block)
    def _(index):
        here = pl.ds(pl.multiple_of(index * block, block), block)
        y_ref[here, :] = mlp_block(x_ref[here, :], up_ref, down_ref)


def mlp_layer(rows, w_up, w_down):
    return pl.pallas_call(
        mlp_kernel,
        out_shape=jax.ShapeDtypeStruct(rows.shape, BF16),
        in_specs=vmem(3),
        out_specs=vmem(1)[0],
        compiler_params=params(rows.shape[0]),
    )(rows, w_up, w_down)


def local(clip_tokens, spatial_qkv, spatial_out, temporal_qkv, temporal_out, mlp_up, mlp_down):
    frame_count, patches, width = clip_tokens.shape
    devices = lax.axis_size("seq")
    share = patches // devices
    frames = frame_count * devices
    mixed = []
    for index in range(frame_count):
        rows, next_qkv, next_out = spatial_layer(
            clip_tokens[index], spatial_qkv, spatial_out, temporal_qkv, temporal_out
        )
        mixed.append(rows)
    mixed = jnp.stack(mixed)
    mixed, mlp_up, mlp_down = lax.optimization_barrier((mixed, mlp_up, mlp_down))
    blocks = mixed.reshape(frame_count, devices, share, width)
    arrived = lax.all_to_all(blocks, "seq", split_axis=1, concat_axis=0, tiled=True)
    tokens = arrived.reshape(frames * share, width)
    after_time = temporal_layer(tokens, next_qkv, next_out, share)
    returned = after_time.reshape(frames, 1, share, width)
    back = lax.all_to_all(returned, "seq", split_axis=0, concat_axis=1, tiled=True)
    result = mlp_layer(back.reshape(frame_count * patches, width), mlp_up, mlp_down)
    return result.reshape(frame_count, patches, width)


def solution(mesh):
    in_specs = (P(("groups", "seq"), None, None), P(), P(), P(), P(), P(), P())
    out_specs = P(("groups", "seq"), None, None)
    return jax.shard_map(local, mesh=mesh, in_specs=in_specs, out_specs=out_specs, check_vma=False)
```

time: 32 us -> 31.5 us (0.984)
  Pallas kernels: 5.95 us -> 5.45 us
    pallas_call x1, Pallas kernels: 2.1 us -> 1.68 us  [mlp_layer(): pl.pallas_call(mlp_kernel, out_shape=jax.ShapeDtypeStruct(rows.shape, BF1...]
where the time goes in v4:
time: 31.5 us; the launch traced here: 31.3 us
  blocking collectives  25.8 us (82%)
  Pallas kernels  5.45 us (17%)
    all_to_all x1, blocking collectives, local(): lax.all_to_all(blocks, 'seq', split_axis=1, concat_axis=0, tiled=True)  15.3 us
    all_to_all x1, blocking collectives, local(): lax.all_to_all(returned, 'seq', split_axis=0, concat_axis=1, tiled=True)  10.5 us
    pallas_call x1, Pallas kernels, spatial_layer(): pl.pallas_call(spatial_kernel, out_shape=[jax.ShapeDtypeStruct((count, wi...  2.68 us
    pallas_call x1, Pallas kernels, mlp_layer(): pl.pallas_call(mlp_kernel, out_shape=jax.ShapeDtypeStruct(rows.shape, BF1...  1.68 us
    pallas_call x1, Pallas kernels, temporal_layer(): pl.pallas_call(functools.partial(temporal_kernel, stride), out_shape=jax....  1.08 us

profile of v4, /device:TPU:0, one launch (start us, length us, event | category | flops | bytes accessed | tf_op | source)
XLA Modules:
  0.0 31.3 jit_solution(8931566872692376540)
XLA Ops:
  0.0 0.0 copy-start.1
  0.0 2.7 %shard_map.73 = (bf16[128,512]{1,0:T(8,128)(2,1)S(1)}, bf16[512,1536]{1,0:T(8,128)(2,1)S(1)}, bf16[512,512]{1,0:T(8,128)(2,1)S(1)}) custom-call(bf16[128,512]{1,0:T(8,128)(2,1)} %bitcast.15, bf16[512,1536]{1,0:T(8,128)(2,1)} %qkv_hbm.1, bf16[512,512]{1,0:T(8,128)(2,1)} %out_hbm.1, bf16[512,1536]{1,0:T(8,128)(2,1)} %next_qkv_hbm.1, bf16[512,512]{1,0:T(8,128)(2,1)} %next_out_hbm.1), custom_call_target="tpu_custom_call" | custom-call | tf_op jit(solution)/shard_map/pallas_call | solution.py:143
  2.7 0.0 copy-start
  2.7 15.3 %all_to_all.8 = bf16[1,16,8,512]{3,2,0,1:T(8,128)(2,1)S(1)} all-to-all(bf16[1,16,8,512]{3,2,0,1:T(8,128)(2,1)S(1)} %bitcast.14), channel_id=1, replica_groups=mesh['groups'=2,'seq'=16] {'seq'}, dimensions={1} | all-to-all | bytes 262144 | tf_op jit(solution)/shard_map/all_to_all | solution.py:231
  18.0 1.1 %shard_map.74 = bf16[128,512]{1,0:T(8,128)(2,1)S(1)} custom-call(bf16[128,512]{1,0:T(8,128)(2,1)S(1)} %bitcast.11, bf16[512,1536]{1,0:T(8,128)(2,1)S(1)} %get-tuple-element.13.qkv_ref, bf16[512,512]{1,0:T(8,128)(2,1)S(1)} %get-tuple-element.14.out_ref), custom_call_target="tpu_custom_call" | custom-call | tf_op jit(solution)/shard_map/pallas_call | solution.py:175
  19.0 10.5 %all_to_all.9 = bf16[16,1,8,512]{3,2,1,0:T(8,128)(2,1)S(1)} all-to-all(bf16[16,1,8,512]{3,2,1,0:T(8,128)(2,1)S(1)} %bitcast.12), channel_id=1, replica_groups=mesh['groups'=2,'seq'=16] {'seq'}, dimensions={0} | all-to-all | bytes 262144 | tf_op jit(solution)/shard_map/all_to_all | solution.py:235
  29.6 0.0 copy-done.1
  29.6 0.0 copy-done
  29.6 1.7 %shard_map.75 = bf16[128,512]{1,0:T(8,128)(2,1)} custom-call(bf16[128,512]{1,0:T(8,128)(2,1)S(1)} %bitcast.13, bf16[512,2048]{1,0:T(8,128)(2,1)S(1)} %copy-done, bf16[2048,512]{1,0:T(8,128)(2,1)S(1)} %copy-done.1), custom_call_target="tpu_custom_call" | custom-call | tf_op jit(solution)/shard_map/pallas_call | solution.py:208
Async XLA Ops:
  0.0 29.6 %copy-start.1 = (bf16[2048,512]{1,0:T(8,128)(2,1)S(1)}, bf16[2048,512]{1,0:T(8,128)(2,1)}, u32[]{:S(2)}) copy-start(bf16[2048,512]{1,0:T(8,128)(2,1)} %down_ref) | copy-start | bytes 6291460
  2.7 26.9 %copy-start = (bf16[512,2048]{1,0:T(8,128)(2,1)S(1)}, bf16[512,2048]{1,0:T(8,128)(2,1)}, u32[]{:S(2)}) copy-start(bf16[512,2048]{1,0:T(8,128)(2,1)} %up_ref) | copy-start | bytes 6291460

commit v5 on v4

--- a/solution.py
+++ b/solution.py
@@ -117,10 +117,10 @@
         return copy
 
     x_copy = fetch(x_hbm, x_ref, 0)
-    copies = []
-    for block in range(3):
-        columns = slice(block * width, (block + 1) * width)
-        copies.append(fetch(qkv_hbm.at[:, columns], qkv_ref.at[:, columns], 1 + block))
+    copies = [
+        fetch(qkv_hbm.at[:, : 2 * width], qkv_ref.at[:, : 2 * width], 1),
+        fetch(qkv_hbm.at[:, 2 * width :], qkv_ref.at[:, 2 * width :], 2),
+    ]
     out_copy = fetch(out_hbm, out_ref, 4)
     next_copies = [
         fetch(next_qkv_hbm, next_qkv_ref, 5), fetch(next_out_hbm, next_out_ref, 6)
@@ -128,12 +128,15 @@
     x_copy.wait()
     x = x_ref[...].astype(F32)
     normed = norm_rows(x)
-    for block, copy in enumerate(copies):
-        columns = slice(block * width, (block + 1) * width)
-        copy.wait()
-        packed_ref[:, columns] = dot(normed, qkv_ref[:, columns]).astype(BF16)
+    copies[0].wait()
+    first = dot(normed, qkv_ref[:, : 2 * width]).astype(BF16)
+    copies[1].wait()
     out_copy.wait()
-    attend_and_project(packed_ref, out_ref, x, y_ref, heads_ref, 0)
+    packed = jnp.concatenate([first, dot(normed, qkv_ref[:, 2 * width :]).astype(BF16)], axis=1)
+    if x.shape[0] > LANES:
+        packed_ref[...] = packed
+        packed = packed_ref
+    attend_and_project(packed, out_ref, x, y_ref, heads_ref, 0)
     for copy in next_copies:
         copy.wait()
 
@@ -214,11 +217,19 @@
     )(rows, w_up, w_down)
 
 
+def middle_first(devices):
+    order = list(range(devices))
+    middle = max(devices // 2 - 2, 0)
+    order[0], order[middle] = order[middle], order[0]
+    return order
+
+
 def local(clip_tokens, spatial_qkv, spatial_out, temporal_qkv, temporal_out, mlp_up, mlp_down):
     frame_count, patches, width = clip_tokens.shape
     devices = lax.axis_size("seq")
     share = patches // devices
     frames = frame_count * devices
+    order = middle_first(devices)
     mixed = []
     for index in range(frame_count):
         rows, next_qkv, next_out = spatial_layer(
@@ -228,11 +239,15 @@
     mixed = jnp.stack(mixed)
     mixed, mlp_up, mlp_down = lax.optimization_barrier((mixed, mlp_up, mlp_down))
     blocks = mixed.reshape(frame_count, devices, share, width)
-    arrived = lax.all_to_all(blocks, "seq", split_axis=1, concat_axis=0, tiled=True)
+    arrived = lax.all_to_all(
+        blocks, "seq", split_axis=1, concat_axis=0, axis_index_groups=[order], tiled=True
+    )
     tokens = arrived.reshape(frames * share, width)
     after_time = temporal_layer(tokens, next_qkv, next_out, share)
     returned = after_time.reshape(frames, 1, share, width)
-    back = lax.all_to_all(returned, "seq", split_axis=0, concat_axis=1, tiled=True)
+    back = lax.all_to_all(
+        returned, "seq", split_axis=0, concat_axis=1, axis_index_groups=[order], tiled=True
+    )
     result = mlp_layer(back.reshape(frame_count * patches, width), mlp_up, mlp_down)
     return result.reshape(frame_count, patches, width)
 

time: 31.5 us -> 27.1 us (0.86)
  blocking collectives: 25.8 us -> 21.6 us
    all_to_all x2, blocking collectives: 25.8 us -> 21.6 us  [the longest x1 12.6 us: local(): lax.all_to_all(blocks, 'seq', split_axis=1, concat_axis=0, axis_index_gro...]
where the time goes in v5:
time: 27.1 us; the launch traced here: 26.9 us
  blocking collectives  21.6 us (80%)
  Pallas kernels  5.3 us (20%)
    all_to_all x1, blocking collectives, local(): lax.all_to_all(blocks, 'seq', split_axis=1, concat_axis=0, axis_index_gro...  12.6 us
    all_to_all x1, blocking collectives, local(): lax.all_to_all(returned, 'seq', split_axis=0, concat_axis=1, axis_index_g...  8.93 us
    pallas_call x1, Pallas kernels, spatial_layer(): pl.pallas_call(spatial_kernel, out_shape=[jax.ShapeDtypeStruct((count, wi...  2.55 us
    pallas_call x1, Pallas kernels, mlp_layer(): pl.pallas_call(mlp_kernel, out_shape=jax.ShapeDtypeStruct(rows.shape, BF1...  1.67 us
    pallas_call x1, Pallas kernels, temporal_layer(): pl.pallas_call(functools.partial(temporal_kernel, stride), out_shape=jax....  1.08 us

profile of v5, /device:TPU:0, one launch (start us, length us, event | category | flops | bytes accessed | tf_op | source)
XLA Modules:
  0.0 26.9 jit_solution(859835679147965087)
XLA Ops:
  0.0 0.0 copy-start.1
  0.0 2.5 %shard_map.73 = (bf16[128,512]{1,0:T(8,128)(2,1)S(1)}, bf16[512,1536]{1,0:T(8,128)(2,1)S(1)}, bf16[512,512]{1,0:T(8,128)(2,1)S(1)}) custom-call(bf16[128,512]{1,0:T(8,128)(2,1)} %bitcast.15, bf16[512,1536]{1,0:T(8,128)(2,1)} %qkv_hbm.1, bf16[512,512]{1,0:T(8,128)(2,1)} %out_hbm.1, bf16[512,1536]{1,0:T(8,128)(2,1)} %next_qkv_hbm.1, bf16[512,512]{1,0:T(8,128)(2,1)} %next_out_hbm.1), custom_call_target="tpu_custom_call" | custom-call | tf_op jit(solution)/shard_map/pallas_call | solution.py:146
  2.6 0.0 copy-start
  2.6 12.6 %all_to_all.8 = bf16[1,16,8,512]{3,2,0,1:T(8,128)(2,1)S(1)} all-to-all(bf16[1,16,8,512]{3,2,0,1:T(8,128)(2,1)S(1)} %bitcast.14), channel_id=1, replica_groups={{6,1,2,3,4,5,0,7,8,9,10,11,12,13,14,15},{22,17,18,19,20,21,16,23,24,25,..., dimensions={1} | all-to-all | bytes 262144 | tf_op jit(solution)/shard_map/all_to_all | solution.py:242
  15.2 1.1 %shard_map.74 = bf16[128,512]{1,0:T(8,128)(2,1)S(1)} custom-call(bf16[128,512]{1,0:T(8,128)(2,1)S(1)} %bitcast.11, bf16[512,1536]{1,0:T(8,128)(2,1)S(1)} %get-tuple-element.13.qkv_ref, bf16[512,512]{1,0:T(8,128)(2,1)S(1)} %get-tuple-element.14.out_ref), custom_call_target="tpu_custom_call" | custom-call | tf_op jit(solution)/shard_map/pallas_call | solution.py:178
  16.3 8.9 %all_to_all.9 = bf16[16,1,8,512]{3,2,1,0:T(8,128)(2,1)S(1)} all-to-all(bf16[16,1,8,512]{3,2,1,0:T(8,128)(2,1)S(1)} %bitcast.12), channel_id=1, replica_groups={{6,1,2,3,4,5,0,7,8,9,10,11,12,13,14,15},{22,17,18,19,20,21,16,23,24,25,..., dimensions={0} | all-to-all | bytes 262144 | tf_op jit(solution)/shard_map/all_to_all | solution.py:248
  25.2 0.0 copy-done.1
  25.2 0.0 copy-done
  25.2 1.7 %shard_map.75 = bf16[128,512]{1,0:T(8,128)(2,1)} custom-call(bf16[128,512]{1,0:T(8,128)(2,1)S(1)} %bitcast.13, bf16[512,2048]{1,0:T(8,128)(2,1)S(1)} %copy-done, bf16[2048,512]{1,0:T(8,128)(2,1)S(1)} %copy-done.1), custom_call_target="tpu_custom_call" | custom-call | tf_op jit(solution)/shard_map/pallas_call | solution.py:211
Async XLA Ops:
  0.0 25.2 %copy-start.1 = (bf16[2048,512]{1,0:T(8,128)(2,1)S(1)}, bf16[2048,512]{1,0:T(8,128)(2,1)}, u32[]{:S(2)}) copy-start(bf16[2048,512]{1,0:T(8,128)(2,1)} %down_ref) | copy-start | bytes 6291460
  2.6 22.7 %copy-start = (bf16[512,2048]{1,0:T(8,128)(2,1)S(1)}, bf16[512,2048]{1,0:T(8,128)(2,1)}, u32[]{:S(2)}) copy-start(bf16[512,2048]{1,0:T(8,128)(2,1)} %up_ref) | copy-start | bytes 6291460

commit v6 on v5

--- a/solution.py
+++ b/solution.py
@@ -2,6 +2,7 @@
 
 import jax
 import jax.numpy as jnp
+import numpy as np
 from jax import lax
 from jax.experimental import pallas as pl
 from jax.experimental.pallas import tpu as pltpu
@@ -217,10 +218,10 @@
     )(rows, w_up, w_down)
 
 
-def middle_first(devices):
-    order = list(range(devices))
-    middle = max(devices // 2 - 2, 0)
-    order[0], order[middle] = order[middle], order[0]
+def exchange_order(devices):
+    order = np.random.RandomState(0).permutation(devices).tolist()
+    first = order.index(min(devices // 2 + 3, devices - 1))
+    order[0], order[first] = order[first], order[0]
     return order
 
 
@@ -229,7 +230,7 @@
     devices = lax.axis_size("seq")
     share = patches // devices
     frames = frame_count * devices
-    order = middle_first(devices)
+    order = exchange_order(devices)
     mixed = []
     for index in range(frame_count):
         rows, next_qkv, next_out = spatial_layer(

time: 27.1 us -> 26.5 us (0.978)
  blocking collectives: 21.6 us -> 21 us
    all_to_all x1, blocking collectives: 12.6 us -> 11.6 us  [local(): lax.all_to_all(blocks, 'seq', split_axis=1, concat_axis=0, axis_index_gro...]
    all_to_all x1, blocking collectives: 8.93 us -> 9.37 us  [local(): lax.all_to_all(returned, 'seq', split_axis=0, concat_axis=1, axis_index_g...]
where the time goes in v6:
time: 26.5 us; the launch traced here: 26.3 us
  blocking collectives  21 us (79%)
  Pallas kernels  5.3 us (20%)
    all_to_all x1, blocking collectives, local(): lax.all_to_all(blocks, 'seq', split_axis=1, concat_axis=0, axis_index_gro...  11.6 us
    all_to_all x1, blocking collectives, local(): lax.all_to_all(returned, 'seq', split_axis=0, concat_axis=1, axis_index_g...  9.37 us
    pallas_call x1, Pallas kernels, spatial_layer(): pl.pallas_call(spatial_kernel, out_shape=[jax.ShapeDtypeStruct((count, wi...  2.55 us
    pallas_call x1, Pallas kernels, mlp_layer(): pl.pallas_call(mlp_kernel, out_shape=jax.ShapeDtypeStruct(rows.shape, BF1...  1.67 us
    pallas_call x1, Pallas kernels, temporal_layer(): pl.pallas_call(functools.partial(temporal_kernel, stride), out_shape=jax....  1.08 us

profile of v6, /device:TPU:0, one launch (start us, length us, event | category | flops | bytes accessed | tf_op | source)
XLA Modules:
  0.0 26.3 jit_solution(5102913718204693834)
XLA Ops:
  0.0 0.0 copy-start.1
  0.0 2.5 %shard_map.73 = (bf16[128,512]{1,0:T(8,128)(2,1)S(1)}, bf16[512,1536]{1,0:T(8,128)(2,1)S(1)}, bf16[512,512]{1,0:T(8,128)(2,1)S(1)}) custom-call(bf16[128,512]{1,0:T(8,128)(2,1)} %bitcast.15, bf16[512,1536]{1,0:T(8,128)(2,1)} %qkv_hbm.1, bf16[512,512]{1,0:T(8,128)(2,1)} %out_hbm.1, bf16[512,1536]{1,0:T(8,128)(2,1)} %next_qkv_hbm.1, bf16[512,512]{1,0:T(8,128)(2,1)} %next_out_hbm.1), custom_call_target="tpu_custom_call" | custom-call | tf_op jit(solution)/shard_map/pallas_call | solution.py:147
  2.6 0.0 copy-start
  2.6 11.6 %all_to_all.8 = bf16[1,16,8,512]{3,2,0,1:T(8,128)(2,1)S(1)} all-to-all(bf16[1,16,8,512]{3,2,0,1:T(8,128)(2,1)S(1)} %bitcast.14), channel_id=1, replica_groups={{11,6,8,9,13,4,2,14,10,7,15,1,3,0,5,12},{27,22,24,25,29,20,18,30,26,23,..., dimensions={1} | all-to-all | bytes 262144 | tf_op jit(solution)/shard_map/all_to_all | solution.py:243
  14.2 1.1 %shard_map.74 = bf16[128,512]{1,0:T(8,128)(2,1)S(1)} custom-call(bf16[128,512]{1,0:T(8,128)(2,1)S(1)} %bitcast.11, bf16[512,1536]{1,0:T(8,128)(2,1)S(1)} %get-tuple-element.13.qkv_ref, bf16[512,512]{1,0:T(8,128)(2,1)S(1)} %get-tuple-element.14.out_ref), custom_call_target="tpu_custom_call" | custom-call | tf_op jit(solution)/shard_map/pallas_call | solution.py:179
  15.2 9.4 %all_to_all.9 = bf16[16,1,8,512]{3,2,1,0:T(8,128)(2,1)S(1)} all-to-all(bf16[16,1,8,512]{3,2,1,0:T(8,128)(2,1)S(1)} %bitcast.12), channel_id=1, replica_groups={{11,6,8,9,13,4,2,14,10,7,15,1,3,0,5,12},{27,22,24,25,29,20,18,30,26,23,..., dimensions={0} | all-to-all | bytes 262144 | tf_op jit(solution)/shard_map/all_to_all | solution.py:249
  24.6 0.0 copy-done.1
  24.6 0.0 copy-done
  24.6 1.7 %shard_map.75 = bf16[128,512]{1,0:T(8,128)(2,1)} custom-call(bf16[128,512]{1,0:T(8,128)(2,1)S(1)} %bitcast.13, bf16[512,2048]{1,0:T(8,128)(2,1)S(1)} %copy-done, bf16[2048,512]{1,0:T(8,128)(2,1)S(1)} %copy-done.1), custom_call_target="tpu_custom_call" | custom-call | tf_op jit(solution)/shard_map/pallas_call | solution.py:212
Async XLA Ops:
  0.0 24.6 %copy-start.1 = (bf16[2048,512]{1,0:T(8,128)(2,1)S(1)}, bf16[2048,512]{1,0:T(8,128)(2,1)}, u32[]{:S(2)}) copy-start(bf16[2048,512]{1,0:T(8,128)(2,1)} %down_ref) | copy-start | bytes 6291460
  2.6 22.1 %copy-start = (bf16[512,2048]{1,0:T(8,128)(2,1)S(1)}, bf16[512,2048]{1,0:T(8,128)(2,1)}, u32[]{:S(2)}) copy-start(bf16[512,2048]{1,0:T(8,128)(2,1)} %up_ref) | copy-start | bytes 6291460

commit v7 on v6

--- a/solution.py
+++ b/solution.py
@@ -219,7 +219,7 @@
 
 
 def exchange_order(devices):
-    order = np.random.RandomState(0).permutation(devices).tolist()
+    order = np.random.RandomState(24).permutation(devices).tolist()
     first = order.index(min(devices // 2 + 3, devices - 1))
     order[0], order[first] = order[first], order[0]
     return order

time: 26.5 us -> 25.9 us (0.977)
  blocking collectives: 21 us -> 20.4 us
    all_to_all x1, blocking collectives: 11.6 us -> 11.3 us  [local(): lax.all_to_all(blocks, 'seq', split_axis=1, concat_axis=0, axis_index_gro...]
where the time goes in v7:
time: 25.9 us; the launch traced here: 25.8 us
  blocking collectives  20.4 us (79%)
  Pallas kernels  5.31 us (21%)
    all_to_all x1, blocking collectives, local(): lax.all_to_all(blocks, 'seq', split_axis=1, concat_axis=0, axis_index_gro...  11.3 us
    all_to_all x1, blocking collectives, local(): lax.all_to_all(returned, 'seq', split_axis=0, concat_axis=1, axis_index_g...  9.16 us
    pallas_call x1, Pallas kernels, spatial_layer(): pl.pallas_call(spatial_kernel, out_shape=[jax.ShapeDtypeStruct((count, wi...  2.55 us
    pallas_call x1, Pallas kernels, mlp_layer(): pl.pallas_call(mlp_kernel, out_shape=jax.ShapeDtypeStruct(rows.shape, BF1...  1.68 us
    pallas_call x1, Pallas kernels, temporal_layer(): pl.pallas_call(functools.partial(temporal_kernel, stride), out_shape=jax....  1.08 us

profile of v7, /device:TPU:0, one launch (start us, length us, event | category | flops | bytes accessed | tf_op | source)
XLA Modules:
  0.0 25.8 jit_solution(363265457967947566)
XLA Ops:
  0.0 0.0 copy-start.1
  0.0 2.5 %shard_map.73 = (bf16[128,512]{1,0:T(8,128)(2,1)S(1)}, bf16[512,1536]{1,0:T(8,128)(2,1)S(1)}, bf16[512,512]{1,0:T(8,128)(2,1)S(1)}) custom-call(bf16[128,512]{1,0:T(8,128)(2,1)} %bitcast.15, bf16[512,1536]{1,0:T(8,128)(2,1)} %qkv_hbm.1, bf16[512,512]{1,0:T(8,128)(2,1)} %out_hbm.1, bf16[512,1536]{1,0:T(8,128)(2,1)} %next_qkv_hbm.1, bf16[512,512]{1,0:T(8,128)(2,1)} %next_out_hbm.1), custom_call_target="tpu_custom_call" | custom-call | tf_op jit(solution)/shard_map/pallas_call | solution.py:147
  2.6 0.0 copy-start
  2.6 11.3 %all_to_all.8 = bf16[1,16,8,512]{3,2,0,1:T(8,128)(2,1)S(1)} all-to-all(bf16[1,16,8,512]{3,2,0,1:T(8,128)(2,1)S(1)} %bitcast.14), channel_id=1, replica_groups={{11,13,9,5,15,12,8,14,4,10,6,1,7,0,3,2},{27,29,25,21,31,28,24,30,20,26,..., dimensions={1} | all-to-all | bytes 262144 | tf_op jit(solution)/shard_map/all_to_all | solution.py:243
  13.8 1.1 %shard_map.74 = bf16[128,512]{1,0:T(8,128)(2,1)S(1)} custom-call(bf16[128,512]{1,0:T(8,128)(2,1)S(1)} %bitcast.11, bf16[512,1536]{1,0:T(8,128)(2,1)S(1)} %get-tuple-element.13.qkv_ref, bf16[512,512]{1,0:T(8,128)(2,1)S(1)} %get-tuple-element.14.out_ref), custom_call_target="tpu_custom_call" | custom-call | tf_op jit(solution)/shard_map/pallas_call | solution.py:179
  14.9 9.2 %all_to_all.9 = bf16[16,1,8,512]{3,2,1,0:T(8,128)(2,1)S(1)} all-to-all(bf16[16,1,8,512]{3,2,1,0:T(8,128)(2,1)S(1)} %bitcast.12), channel_id=1, replica_groups={{11,13,9,5,15,12,8,14,4,10,6,1,7,0,3,2},{27,29,25,21,31,28,24,30,20,26,..., dimensions={0} | all-to-all | bytes 262144 | tf_op jit(solution)/shard_map/all_to_all | solution.py:249
  24.1 0.0 copy-done.1
  24.1 0.0 copy-done
  24.1 1.7 %shard_map.75 = bf16[128,512]{1,0:T(8,128)(2,1)} custom-call(bf16[128,512]{1,0:T(8,128)(2,1)S(1)} %bitcast.13, bf16[512,2048]{1,0:T(8,128)(2,1)S(1)} %copy-done, bf16[2048,512]{1,0:T(8,128)(2,1)S(1)} %copy-done.1), custom_call_target="tpu_custom_call" | custom-call | tf_op jit(solution)/shard_map/pallas_call | solution.py:212
Async XLA Ops:
  0.0 24.1 %copy-start.1 = (bf16[2048,512]{1,0:T(8,128)(2,1)S(1)}, bf16[2048,512]{1,0:T(8,128)(2,1)}, u32[]{:S(2)}) copy-start(bf16[2048,512]{1,0:T(8,128)(2,1)} %down_ref) | copy-start | bytes 6291460
  2.6 21.5 %copy-start = (bf16[512,2048]{1,0:T(8,128)(2,1)S(1)}, bf16[512,2048]{1,0:T(8,128)(2,1)}, u32[]{:S(2)}) copy-start(bf16[512,2048]{1,0:T(8,128)(2,1)} %up_ref) | copy-start | bytes 6291460

commit v8 on v7

--- a/solution.py
+++ b/solution.py
@@ -39,6 +39,17 @@
 
 def dot(left, right):
     return jnp.dot(left, right, preferred_element_type=F32)
+
+
+def norm_dot(x, weights):
+    rows = x.shape[0]
+    stacked = jnp.concatenate([x, jnp.ones((16, x.shape[1]), BF16)], axis=0)
+    product = dot(stacked, weights)
+    values = x.astype(F32)
+    mean = jnp.mean(values, axis=-1, keepdims=True)
+    center = values - mean
+    spread = jnp.mean(center * center, axis=-1, keepdims=True)
+    return (product[:rows] - mean * product[rows : rows + 1]) * lax.rsqrt(spread + 1e-05)
 
 
 def pair_ones(keys, head):
@@ -167,7 +178,7 @@
 
 def temporal_kernel(stride, x_ref, qkv_ref, out_ref, y_ref, packed_ref, heads_ref):
     x = x_ref[...].astype(F32)
-    packed = dot(norm_rows(x), qkv_ref[...]).astype(BF16)
+    packed = norm_dot(x_ref[...], qkv_ref[...]).astype(BF16)
     if x.shape[0] > LANES:
         packed_ref[...] = packed
         packed = packed_ref
@@ -190,8 +201,7 @@
 
 
 def mlp_block(x, up_ref, down_ref):
-    normed = norm_rows(x.astype(F32))
-    u = dot(normed, up_ref[...])
+    u = norm_dot(x, up_ref[...])
     half = 0.5 * u
     bend = jnp.tanh(u * (0.7978845608028654 + 0.035677408136300125 * (u * u)))
     hidden = (half + half * bend).astype(BF16)

time: 25.9 us -> 25.7 us (level)
  Pallas kernels: 5.31 us -> 5.05 us
where the time goes in v8:
time: 25.7 us; the launch traced here: 25.5 us
  blocking collectives  20.4 us (79%)
  Pallas kernels  5.05 us (20%)
    all_to_all x1, blocking collectives, local(): lax.all_to_all(blocks, 'seq', split_axis=1, concat_axis=0, axis_index_gro...  11.3 us
    all_to_all x1, blocking collectives, local(): lax.all_to_all(returned, 'seq', split_axis=0, concat_axis=1, axis_index_g...  9.16 us
    pallas_call x1, Pallas kernels, spatial_layer(): pl.pallas_call(spatial_kernel, out_shape=[jax.ShapeDtypeStruct((count, wi...  2.55 us
    pallas_call x1, Pallas kernels, mlp_layer(): pl.pallas_call(mlp_kernel, out_shape=jax.ShapeDtypeStruct(rows.shape, BF1...  1.51 us
    pallas_call x1, Pallas kernels, temporal_layer(): pl.pallas_call(functools.partial(temporal_kernel, stride), out_shape=jax....  1 us

profile of v8, /device:TPU:0, one launch (start us, length us, event | category | flops | bytes accessed | tf_op | source)
XLA Modules:
  0.0 25.5 jit_solution(14230108877443284798)
XLA Ops:
  0.0 0.0 copy-start.1
  0.0 2.5 %shard_map.73 = (bf16[128,512]{1,0:T(8,128)(2,1)S(1)}, bf16[512,1536]{1,0:T(8,128)(2,1)S(1)}, bf16[512,512]{1,0:T(8,128)(2,1)S(1)}) custom-call(bf16[128,512]{1,0:T(8,128)(2,1)} %bitcast.15, bf16[512,1536]{1,0:T(8,128)(2,1)} %qkv_hbm.1, bf16[512,512]{1,0:T(8,128)(2,1)} %out_hbm.1, bf16[512,1536]{1,0:T(8,128)(2,1)} %next_qkv_hbm.1, bf16[512,512]{1,0:T(8,128)(2,1)} %next_out_hbm.1), custom_call_target="tpu_custom_call" | custom-call | tf_op jit(solution)/shard_map/pallas_call | solution.py:158
  2.6 0.0 copy-start
  2.6 11.3 %all_to_all.8 = bf16[1,16,8,512]{3,2,0,1:T(8,128)(2,1)S(1)} all-to-all(bf16[1,16,8,512]{3,2,0,1:T(8,128)(2,1)S(1)} %bitcast.14), channel_id=1, replica_groups={{11,13,9,5,15,12,8,14,4,10,6,1,7,0,3,2},{27,29,25,21,31,28,24,30,20,26,..., dimensions={1} | all-to-all | bytes 262144 | tf_op jit(solution)/shard_map/all_to_all | solution.py:253
  13.8 1.0 %shard_map.74 = bf16[128,512]{1,0:T(8,128)(2,1)S(1)} custom-call(bf16[128,512]{1,0:T(8,128)(2,1)S(1)} %bitcast.11, bf16[512,1536]{1,0:T(8,128)(2,1)S(1)} %get-tuple-element.13.qkv_ref, bf16[512,512]{1,0:T(8,128)(2,1)S(1)} %get-tuple-element.14.out_ref), custom_call_target="tpu_custom_call" | custom-call | tf_op jit(solution)/shard_map/pallas_call | solution.py:190
  14.8 9.2 %all_to_all.9 = bf16[16,1,8,512]{3,2,1,0:T(8,128)(2,1)S(1)} all-to-all(bf16[16,1,8,512]{3,2,1,0:T(8,128)(2,1)S(1)} %bitcast.12), channel_id=1, replica_groups={{11,13,9,5,15,12,8,14,4,10,6,1,7,0,3,2},{27,29,25,21,31,28,24,30,20,26,..., dimensions={0} | all-to-all | bytes 262144 | tf_op jit(solution)/shard_map/all_to_all | solution.py:259
  24.0 0.0 copy-done.1
  24.0 0.0 copy-done
  24.0 1.5 %shard_map.75 = bf16[128,512]{1,0:T(8,128)(2,1)} custom-call(bf16[128,512]{1,0:T(8,128)(2,1)S(1)} %bitcast.13, bf16[512,2048]{1,0:T(8,128)(2,1)S(1)} %copy-done, bf16[2048,512]{1,0:T(8,128)(2,1)S(1)} %copy-done.1), custom_call_target="tpu_custom_call" | custom-call | tf_op jit(solution)/shard_map/pallas_call | solution.py:222
Async XLA Ops:
  0.0 24.0 %copy-start.1 = (bf16[2048,512]{1,0:T(8,128)(2,1)S(1)}, bf16[2048,512]{1,0:T(8,128)(2,1)}, u32[]{:S(2)}) copy-start(bf16[2048,512]{1,0:T(8,128)(2,1)} %down_ref) | copy-start | bytes 6291460
  2.6 21.4 %copy-start = (bf16[512,2048]{1,0:T(8,128)(2,1)S(1)}, bf16[512,2048]{1,0:T(8,128)(2,1)}, u32[]{:S(2)}) copy-start(bf16[512,2048]{1,0:T(8,128)(2,1)} %up_ref) | copy-start | bytes 6291460
